TPU v7x, 512 devices: a whole 4x8x8 slice. The times are simulated.
512 devices in a mesh: dap: 128 (over z, y_hi, x, core), head: 4 (over y_lo).
Axes of the slice: x: 4, y: 8 (y_hi: 2, y_lo: 4; y = y_hi * 4 + y_lo), z: 8, core: 2. Of those that a mesh axis runs over, the one named last changes fastest.
Arguments:
- alignment_activity: bfloat16 [128, 512, 256], P('dap'), may hold values from -6 to 6
- attend_standard_gain: float32 [256], replicated, may hold values from 0.25 to 1.75
- asking_projector: bfloat16 [256, 256], P(None, 'head'), may hold values from -0.5 to 0.5
- lookup_projector: bfloat16 [256, 256], P(None, 'head'), may hold values from -24 to 24
- content_projector: bfloat16 [256, 256], P(None, 'head'), may hold values from -0.375 to 0.375
- gating_projector: bfloat16 [256, 256], P(None, 'head'), may hold values from -0.75 to 0.75
- attend_result_projector: bfloat16 [256, 256], replicated, may hold values from -3 to 3
- tensor_standard_gain: float32 [256], replicated, may hold values from 0.25 to 1.75
- first_factor_projector: bfloat16 [256, 32], P(None, 'head'), may hold values from -0.375 to 0.375
- second_factor_projector: bfloat16 [256, 32], replicated, may hold values from -0.375 to 0.375
- flattened_to_grid_projector: bfloat16 [1024, 128], replicated, may hold values from -1.5 to 1.5
- grid_result_offset: float32 [128], replicated, may hold values from -3 to 3
Outputs:
- alignment_after_vertical: bfloat16 [128, 512, 256], P('dap')
- residue_grid_delta: bfloat16 [512, 512, 128], P(None, 'dap', 'head')
All inputs are finite; a program needn't handle non-finite values.
Results may differ from a plain program's by a relative error of at most 0.018.
Values may be sent and summed in bfloat16 or wider, within the bound.
A program may use at most 64 MiB of HBM per device.

v0:
```python
import jax
import jax.numpy as jnp
from jax import lax
from jax.sharding import PartitionSpec as P

HEAD_DIMENSION = 32
SLAB_DEV = 4


EPS = 1e-05


def standardize_features(values_in, gain):
    values_in = values_in.astype(jnp.float32)
    mean = jnp.mean(values_in, axis=-1, keepdims=True)
    centred = values_in - mean
    variance = jnp.mean(centred * centred, axis=-1, keepdims=True)
    return centred * lax.rsqrt(variance + EPS) * gain


def apply_projection_fn(
    standardized_sequences,
    asking_projector,
    lookup_projector,
    content_projector,
    gating_projector,
    attend_heads_list,
):
    leading_dims = standardized_sequences.shape[:-1]

    def apply_weight(coefficient_array):
        return jnp.dot(
            standardized_sequences, coefficient_array, preferred_element_type=jnp.float32
        ).reshape(leading_dims + (attend_heads_list, HEAD_DIMENSION))

    query = apply_weight(asking_projector).astype(jnp.bfloat16)
    keys = apply_weight(lookup_projector).astype(jnp.bfloat16)
    values = apply_weight(content_projector).astype(jnp.bfloat16)
    gate = jax.nn.sigmoid(apply_weight(gating_projector)).astype(jnp.bfloat16)
    return jnp.concatenate([query, keys, values, gate], axis=-1)


def attend_column(block):
    query = block[..., :HEAD_DIMENSION]
    keys = block[..., HEAD_DIMENSION : 2 * HEAD_DIMENSION]
    values = block[..., 2 * HEAD_DIMENSION : 3 * HEAD_DIMENSION]
    gate = block[..., 3 * HEAD_DIMENSION :]
    scores = jnp.einsum(
        "shd,thd->hst", query, keys, preferred_element_type=jnp.float32
    ) * HEAD_DIMENSION ** (-0.5)
    peak = jnp.max(scores, axis=-1, keepdims=True)
    weights = jnp.exp(scores - peak)
    probs = (weights / jnp.sum(weights, axis=-1, keepdims=True)).astype(jnp.bfloat16)
    mixed = jnp.einsum("hst,thd->shd", probs, values, preferred_element_type=jnp.float32)
    return (mixed * gate.astype(jnp.float32)).astype(jnp.bfloat16)


def attend_all(stacked_tensor):
    columns = jnp.moveaxis(stacked_tensor, 1, 0)
    return jnp.moveaxis(lax.map(attend_column, columns), 0, 1)


def back_rows(mixed):
    return lax.all_to_all(mixed, "dap", split_axis=0, concat_axis=1, tiled=True)


def attend_and_return(block):
    return back_rows(attend_all(block))


def shards(
    alignment_activity,
    attend_standard_gain,
    asking_projector,
    lookup_projector,
    content_projector,
    gating_projector,
    attend_result_projector,
    tensor_standard_gain,
    first_factor_projector,
    second_factor_projector,
    flattened_to_grid_projector,
    grid_result_offset,
):
    attend_heads_list = asking_projector.shape[1] // HEAD_DIMENSION
    standardized_sequences = standardize_features(alignment_activity, attend_standard_gain).astype(
        jnp.bfloat16
    )
    stacked_tensor = apply_projection_fn(
        standardized_sequences,
        asking_projector,
        lookup_projector,
        content_projector,
        gating_projector,
        attend_heads_list,
    )
    mixed = attend_and_return(
        lax.all_to_all(stacked_tensor, "dap", split_axis=1, concat_axis=0, tiled=True)
    )
    flat = mixed.reshape(mixed.shape[0], mixed.shape[1], attend_heads_list * HEAD_DIMENSION)
    rows = attend_result_projector
    grid_increment = jnp.einsum(
        "snc,cd->snd",
        lax.all_gather(flat, "head", axis=2, tiled=True),
        rows,
        preferred_element_type=jnp.float32,
    )
    alignment_after_vertical = (alignment_activity.astype(jnp.float32) + grid_increment).astype(
        jnp.bfloat16
    )
    second_standardized_sequences = standardize_features(
        alignment_after_vertical, tensor_standard_gain
    ).astype(jnp.bfloat16)
    first_factor = jnp.dot(
        second_standardized_sequences, first_factor_projector, preferred_element_type=jnp.float32
    ).astype(jnp.bfloat16)
    second_factor = jnp.dot(
        second_standardized_sequences, second_factor_projector, preferred_element_type=jnp.float32
    ).astype(jnp.bfloat16)
    right_cols = lax.all_to_all(second_factor, "dap", split_axis=1, concat_axis=0, tiled=True)
    slab = SLAB_DEV * lax.axis_size("dap")
    total_seqs = right_cols.shape[0]
    right_width = second_factor.shape[2]
    own_width = first_factor.shape[2]
    rows = right_cols
    outer_sum = jnp.einsum(
        "sic,sje->ijce",
        lax.all_gather(first_factor, "dap", axis=0, tiled=True),
        rows,
        preferred_element_type=jnp.float32,
    )
    outer = (outer_sum / total_seqs).astype(jnp.bfloat16)
    pair_rows_own = lax.dynamic_slice_in_dim(
        flattened_to_grid_projector,
        lax.axis_index("head") * own_width * right_width,
        own_width * right_width,
        0,
    )
    partial_value = jnp.dot(
        outer.reshape(slab, right_cols.shape[1], own_width * right_width),
        pair_rows_own,
        preferred_element_type=jnp.float32,
    )
    summed = lax.psum_scatter(
        partial_value.astype(jnp.bfloat16), "head", scatter_dimension=2, tiled=True
    ).astype(jnp.float32)
    channel_width = summed.shape[2]
    bias_own = lax.dynamic_slice_in_dim(
        grid_result_offset, lax.axis_index("head") * channel_width, channel_width, 0
    )
    residue_grid_delta = (summed + bias_own).astype(jnp.bfloat16)
    return (alignment_after_vertical, residue_grid_delta)


def solution(mesh):
    placed = (
        P("dap", None, None),
        P(),
        P(None, "head"),
        P(None, "head"),
        P(None, "head"),
        P(None, "head"),
        P(),
        P(),
        P(None, "head"),
        P(),
        P(),
        P(),
    )
    return jax.shard_map(
        shards,
        mesh=mesh,
        in_specs=placed,
        out_specs=(P("dap", None, None), P(None, "dap", "head")),
        check_vma=False,
    )
```

profile of v0, /device:TPU:1, one launch (start us, length us, event | category | flops | bytes accessed | tf_op | source)
XLA Modules:
  0.0 230.8 jit_solution(2580121631120465586)
XLA Ops:
  7.2 1.1 copy.42
  9.1 0.2 fusion.25
  9.3 0.3 fusion.26
  9.6 0.9 copy.47
  10.5 20.9 %all-to-all-start = ((bf16[1,512,2,128]{3,2,0,1:T(2,128)(2,1)}), bf16[1,512,2,128]{3,2,0,1:T(2,128)(2,1)S(1)}, u32[]{:S(2)}, u32[]{:S(2)}) async-start(bf16[1,512,2,128]{3,2,0,1:T(2,128)(2,1)} %copy.47), calls=%async_computation | async-start | bytes 524288 | tf_op jit(solution)/shard_map/all_to_all | solution.py:98
  31.5 16.1 %all-to-all-done = bf16[1,512,2,128]{3,2,0,1:T(2,128)(2,1)S(1)} async-done(((bf16[1,512,2,128]{3,2,0,1:T(2,128)(2,1)}), bf16[1,512,2,128]{3,2,0,1:T(2,128)(2,1)S(1)}, u32[]{:S(2)}, u32[]{:S(2)}) %all-to-all-start) | async-done | bytes 262176 | tf_op jit(solution)/shard_map/all_to_all | solution.py:98
  47.8 2.8 %while.10 = (s32[]{:T(128)}, bf16[4,128,2,32]{1,3,2,0:T(8,128)(2,1)S(1)}, bf16[4,128,2,128]{1,3,2,0:T(8,128)(2,1)S(1)}, s32[]{:T(128)}) while((s32[]{:T(128)}, bf16[4,128,2,32]{1,3,2,0:T(8,128)(2,1)S(1)}, bf16[4,128,2,128]{1,3,2,0:T(8,128)(2,1)S(1)}, s32[]{:T(128)}) %tuple.28), condition=%wide.region_5.6_spmd, body=%wide.region_2.5_spmd.sunk | while | flops 6545920 | bytes 641085 | solution.py:60
  48.0 0.3 fusion.81
  48.7 0.3 fusion.81
  49.5 0.3 fusion.81
  50.2 0.3 fusion.81
  51.0 21.4 %all_to_all.33 = bf16[128,2,128]{2,1,0:T(2,128)(2,1)S(1)} all-to-all(bf16[128,2,128]{2,1,0:T(2,128)(2,1)S(1)} %reshape.132), channel_id=1, replica_groups=mesh['dap'=128,'head'=4] {'dap'}, dimensions={0} | all-to-all | bytes 131072 | tf_op jit(solution)/shard_map/all_to_all | solution.py:64
  72.9 11.0 %all_gather.6 = bf16[1,512,256]{1,2,0:T(8,128)(2,1)S(1)} all-gather(bf16[1,512,64]{1,2,0:T(8,128)(2,1)S(1)} %copy.51), channel_id=1, replica_groups=mesh['dap'=128,'head'=4] {'head'}, dimensions={2}, use_global_device_ids=true | all-gather | bytes 327680 | tf_op jit(solution)/shard_map/all_gather | solution.py:104
  83.8 0.3 convert_reduce_fusion.1
  84.3 0.8 convolution_convert_fusion.5
  85.3 0.9 copy.52
  86.2 9.0 %all-to-all-start.2 = ((bf16[1,512,32]{2,0,1:T(2,128)(2,1)}), bf16[1,512,32]{2,0,1:T(2,128)(2,1)S(1)}, u32[]{:S(2)}, u32[]{:S(2)}) async-start(bf16[1,512,32]{2,0,1:T(2,128)(2,1)} %copy.52), calls=%async_computation.2 | async-start | bytes 524288 | tf_op jit(solution)/shard_map/all_to_all | solution.py:120
  95.3 16.3 %all-to-all-done.2 = bf16[1,512,32]{2,0,1:T(2,128)(2,1)S(1)} async-done(((bf16[1,512,32]{2,0,1:T(2,128)(2,1)}), bf16[1,512,32]{2,0,1:T(2,128)(2,1)S(1)}, u32[]{:S(2)}, u32[]{:S(2)}) %all-to-all-start.2) | async-done | bytes 32800 | tf_op jit(solution)/shard_map/all_to_all | solution.py:120
  111.6 83.6 %all-gather.3.cloned.1.call-done = bf16[65536,8]{0,1:T(8,128)(2,1)} async-done(((bf16[512,8]{0,1:T(8,128)(2,1)}), bf16[65536,8]{0,1:T(8,128)(2,1)}) %all-gather.3.cloned.1.call-update) | async-done | bytes 1048592 | tf_op jit(solution)/shard_map/all_gather | solution.py:128
  195.2 2.1 multiply_convert_fusion
  197.4 1.1 convolution_convert_fusion
  198.6 0.8 copy.57
  199.5 22.9 %reduce-scatter.2.cloned.1.call-done = bf16[512,4,32]{0,2,1:T(8,128)(2,1)} async-done(((bf16[512,4,128]{0,2,1:T(8,128)(2,1)}), bf16[512,4,32]{0,2,1:T(8,128)(2,1)}) %reduce-scatter.2.cloned.1.call-update) | async-done | bytes 131088 | tf_op jit(solution)/shard_map/reduce_scatter | solution.py:144
  222.3 1.6 add_convert_fusion
  (59 shorter events, 3.9 us)
Async XLA Ops:
  7.2 190.2 %copy-start = (bf16[1024,128]{1,0:T(8,128)(2,1)S(1)}, bf16[1024,128]{1,0:T(8,128)(2,1)}, u32[]{:S(2)}) copy-start(bf16[1024,128]{1,0:T(8,128)(2,1)} %param.24) | copy-start | bytes 786436
  7.2 1.4 copy-start.2
  7.2 1.4 copy-start.8
  7.2 1.6 copy-start.3
  7.2 1.9 copy-start.4
  8.4 0.9 copy-start.5
  10.5 37.0 %all-to-all-start = ((bf16[1,512,2,128]{3,2,0,1:T(2,128)(2,1)}), bf16[1,512,2,128]{3,2,0,1:T(2,128)(2,1)S(1)}, u32[]{:S(2)}, u32[]{:S(2)}) async-start(bf16[1,512,2,128]{3,2,0,1:T(2,128)(2,1)} %copy.47), calls=%async_computation | async-start | bytes 524288 | tf_op jit(solution)/shard_map/all_to_all | solution.py:98
  31.4 163.8 %all-gather.3.cloned.1.call-start = ((), (), s32[]{:S(2)}) async-start(), calls=%async_computation.5 | async-start | bytes 1056768 | tf_op jit(solution)/shard_map/all_gather | solution.py:128
  50.6 33.2 %copy-start.1 = (bf16[256,256]{1,0:T(8,128)(2,1)S(1)}, bf16[256,256]{1,0:T(8,128)(2,1)}, u32[]{:S(2)}) copy-start(bf16[256,256]{1,0:T(8,128)(2,1)} %param.20) | copy-start | bytes 393220
  72.6 11.7 %copy-start.7 = (bf16[256,8]{0,1:T(8,128)(2,1)S(1)}, bf16[256,8]{0,1:T(8,128)(2,1)}, u32[]{:S(2)}) copy-start(bf16[256,8]{0,1:T(8,128)(2,1)} %param.22) | copy-start | bytes 12292
  72.6 11.7 %copy-start.9 = (f32[256]{0:T(256)S(1)}, f32[256]{0:T(256)}, u32[]{:S(2)}) copy-start(f32[256]{0:T(256)} %param.21) | copy-start | bytes 3076
  72.9 12.2 %copy-start.6 = (bf16[256,32]{0,1:T(8,128)(2,1)S(1)}, bf16[256,32]{0,1:T(8,128)(2,1)}, u32[]{:S(2)}) copy-start(bf16[256,32]{0,1:T(8,128)(2,1)} %param.23) | copy-start | bytes 49156
  86.2 25.4 %all-to-all-start.2 = ((bf16[1,512,32]{2,0,1:T(2,128)(2,1)}), bf16[1,512,32]{2,0,1:T(2,128)(2,1)S(1)}, u32[]{:S(2)}, u32[]{:S(2)}) async-start(bf16[1,512,32]{2,0,1:T(2,128)(2,1)} %copy.52), calls=%async_computation.2 | async-start | bytes 524288 | tf_op jit(solution)/shard_map/all_to_all | solution.py:120
  95.2 127.1 %reduce-scatter.2.cloned.1.call-start = ((), (), s32[]{:S(2)}) async-start(), calls=%async_computation.4 | async-start | bytes 655360 | tf_op jit(solution)/shard_map/reduce_scatter | solution.py:144
  197.4 1.2 copy-start.10
Sparse Core Ops, SparseCore 0:
  85.2 109.9 all-gather.2
  198.6 23.6 reduce-scatter.1
where the time goes:
time: 232 us; the launch traced here: 231 us
  waiting for transfers between devices  139 us (60%)
  blocking collectives  32.4 us (14%)
  starting transfers between devices  30 us (13%)
  between operations  14.3 us (6%)
  matrix products  8.24 us (4%)
  local copies, waits for them, and re-layouts  4.93 us (2%)
    all_gather x1, waiting for transfers between devices, shards(): lax.all_gather(first_factor, 'dap', axis=0, tiled=True)  83.6 us
    reduce_scatter x1, waiting for transfers between devices, shards(): lax.psum_scatter(partial_value.astype(jnp.bfloat16), 'head', scatter_dime...  22.9 us
    all_to_all x1, blocking collectives, back_rows(): return lax.all_to_all(mixed, 'dap', split_axis=0, concat_axis=1, tiled=True)  21.4 us
    all_to_all x1, starting transfers between devices, shards(): lax.all_to_all(stacked_tensor, 'dap', split_axis=1, concat_axis=0, tiled=...  20.9 us
    all_to_all x1, waiting for transfers between devices, shards(): lax.all_to_all(second_factor, 'dap', split_axis=1, concat_axis=0, tiled=T...  16.3 us
    all_to_all x1, waiting for transfers between devices, shards(): lax.all_to_all(stacked_tensor, 'dap', split_axis=1, concat_axis=0, tiled=...  16.1 us
    all_gather x1, blocking collectives, shards(): lax.all_gather(flat, 'head', axis=2, tiled=True)  11 us
    all_to_all x1, starting transfers between devices, shards(): lax.all_to_all(second_factor, 'dap', split_axis=1, concat_axis=0, tiled=T...  9.03 us
  transfers between devices with their start and end apart: 4, of which 4 were waited for; matrix products, arithmetic and copies ran while one was open for 1% of the time, Pallas kernels for 0%

commit v1 on v0

v1 whole, which is shorter than its diff:
```python
import functools

import jax
import jax.numpy as jnp
from jax import lax
from jax.experimental import pallas as pl
from jax.experimental.pallas import tpu as pltpu
from jax.sharding import PartitionSpec as P

MESH = pl.DeviceIdType.MESH
HEAD_DIMENSION = 32
XC = 8
EPS = 1e-05
BF = jnp.bfloat16
F32 = jnp.float32


def dot(a, b, ca, cb):
    return lax.dot_general(a, b, (((ca,), (cb,)), ((), ())), preferred_element_type=F32)


def standardize(v, gain):
    mean = jnp.mean(v, axis=-1, keepdims=True)
    centred = v - mean
    variance = jnp.mean(centred * centred, axis=-1, keepdims=True)
    return (centred * lax.rsqrt(variance + EPS) * gain).astype(BF)


def swap(src, tmp, dst):
    a, b, width = src.shape
    for i in range(width // 128):
        lanes = slice(i * 128, (i + 1) * 128)
        tmp[i] = src[:, :, lanes].astype(F32).reshape(a * b, 128)
        for k in range(b):
            dst[k, :, lanes] = tmp[i, pl.ds(k, a, stride=b), :].astype(BF)


def kernel(
    dims,
    x_ref, wq_ref, wk_ref, wv_ref, wg_ref, wo_ref, gain1_ref, gain2_ref, f1_ref, f2_ref, pw_ref, bias_ref,
    o0_ref, o1_ref,
    wsend, wall, s2t, r1, tmp, s2, r2, acol, lcol, rcol, l1, tmpl, left, right, z, res, ra1, tmpa, sa2,
    sem_s1, sem_r1, sem_sw, sem_rw, sem_s2, sem_r2, sem_sl1, sem_rl1, sem_sl2, sem_rl2, sem_sl3, sem_rl3,
    sem_sr, sem_rr, sem_sa1, sem_ra1, sem_sa2, sem_ra2, sem_sa3, sem_ra3, sem_sx, sem_rx, sem_loc,
):
    G, H, CM = dims
    X = XC // 2
    S = G * XC
    HW = wq_ref.shape[1]
    NH = HW // HEAD_DIMENSION
    FC = f1_ref.shape[1]
    CC = f2_ref.shape[1]
    CZ = pw_ref.shape[1]
    ZQ = CZ // H
    d = lax.axis_index("dap")
    h = lax.axis_index("head")
    g = d // XC
    xc = d % XC
    xx = xc // 2
    core = xc % 2

    def rcopy(src, dst, ssem, rsem, dd, hh):
        return pltpu.make_async_remote_copy(
            src_ref=src, dst_ref=dst, send_sem=ssem, recv_sem=rsem, device_id=(dd, hh), device_id_type=MESH
        )

    def each(n, f):
        def step(o, c):
            f(o)
            return c

        lax.fori_loop(1, n, step, 0)

    def dg(o):
        return ((g + o) % G) * XC + xc

    def dxc(o):
        return g * XC + (xc + o) % XC

    m = XC * h + xc
    xc_d = m // H
    slot = m % H
    own_writer = xc_d == xc

    barrier = pltpu.get_barrier_semaphore()

    def signal(dd, hh):
        pl.semaphore_signal(barrier, inc=1, device_id=(dd, hh), device_id_type=MESH)

    each(G, lambda o: signal(dg(o), h))
    each(XC, lambda o: signal(dxc(o), h))
    each(H, lambda o: signal(d, (h + o) % H))
    for k in range(H):
        ms = H * xc + k
        src_h, src_xc = ms // XC, ms % XC

        @pl.when(jnp.logical_not((src_h == h) & (src_xc == xc)))
        def _():
            signal(g * XC + src_xc, src_h)

    for i, w in enumerate((wq_ref, wk_ref, wv_ref, wg_ref)):
        wsend[i * HW : (i + 1) * HW, :] = w[...].astype(F32).T.astype(BF)
    f1t = jnp.concatenate([f1_ref[...].astype(F32), jnp.zeros((CM, 128 - FC), F32)], axis=1).T
    wsend[4 * HW :, :] = f1t[:16].astype(BF)
    s2t[...] = jnp.concatenate([f2_ref[...].astype(F32), jnp.zeros((CM, 128 - CC), F32)], axis=1).T[:CC].astype(BF)

    pl.semaphore_wait(barrier, (G - 1) + (XC - 1) + (H - 1) + H - jnp.where(own_writer, 1, 0))

    def a1(o):
        gg = (g + o) % G
        return rcopy(x_ref.at[gg, h], r1.at[g], sem_s1.at[gg], sem_r1.at[g], dg(o), h)

    each(G, lambda o: a1(o).start())
    loc1 = pltpu.make_async_copy(x_ref.at[g, h], r1.at[g], sem_loc.at[0])
    loc1.start()

    def aw(o):
        hh = (h + o) % H
        return rcopy(wsend, wall.at[h], sem_sw.at[hh], sem_rw.at[h], d, hh)

    each(H, lambda o: aw(o).start())
    loc2 = pltpu.make_async_copy(wsend, wall.at[h], sem_loc.at[1])
    loc2.start()

    def wait_r1(o):
        gg = (g + o) % G
        rcopy(x_ref.at[gg, h], r1.at[gg], sem_s1.at[gg], sem_r1.at[gg], dg(o), h).wait_recv()

    loc1.wait()
    each(G, wait_r1)

    swap(r1, tmp, s2)

    def a2(o):
        t = (xc + o) % XC
        rows = pl.ds(pl.multiple_of(xc * G, G), G)
        return rcopy(s2.at[t], r2.at[rows], sem_s2.at[t], sem_r2.at[xc], dxc(o), h)

    each(XC, lambda o: a2(o).start())
    r2[pl.ds(pl.multiple_of(xc * G, G), G), :] = s2[xc]

    def wait_r2(o):
        t = (xc + o) % XC
        rows = pl.ds(pl.multiple_of(t * G, G), G)
        rcopy(s2.at[t], r2.at[rows], sem_s2.at[t], sem_r2.at[t], dxc(o), h).wait_recv()

    each(XC, wait_r2)
    activity = r2[...].astype(F32)
    normed = standardize(activity, gain1_ref[...])

    def wait_w(o):
        hh = (h + o) % H
        rcopy(wsend, wall.at[hh], sem_sw.at[hh], sem_rw.at[hh], d, hh).wait_recv()

    loc2.wait()
    each(H, wait_w)

    mixed = []
    for hp in range(H):
        proj = dot(wall[hp, : 4 * HW, :], normed, 1, 1)
        query = proj[:HW].astype(BF)
        keys = proj[HW : 2 * HW].astype(BF)
        values = proj[2 * HW : 3 * HW].astype(BF)
        gate = jax.nn.sigmoid(proj[3 * HW :]).astype(BF).astype(F32)
        for e in range(NH):
            rows = slice(e * HEAD_DIMENSION, (e + 1) * HEAD_DIMENSION)
            scores = dot(keys[rows], query[rows], 0, 0) * HEAD_DIMENSION ** (-0.5)
            weights = jnp.exp(scores - jnp.max(scores, axis=0, keepdims=True))
            probs = (weights / jnp.sum(weights, axis=0, keepdims=True)).astype(BF)
            mixed.append((dot(values[rows], probs, 1, 0) * gate[rows]).astype(BF))
    mixed = jnp.concatenate(mixed, axis=0)
    after = (activity + dot(mixed, wo_ref[...], 0, 0)).astype(BF)
    acol[...] = after
    normed2 = standardize(after.astype(F32), gain2_ref[...])
    f1 = jnp.concatenate([wall[hp, 4 * HW :, :].astype(F32)[:FC] for hp in range(H)], axis=0).astype(BF)
    lcol[...] = dot(f1, normed2, 1, 1).astype(BF)
    rcol[...] = dot(s2t[...], normed2, 1, 1).astype(BF)

    def al1(o):
        gg = (g + o) % G
        return rcopy(lcol, l1.at[g], sem_sl1.at[gg], sem_rl1.at[g], dg(o), h)

    each(G, lambda o: al1(o).start())
    l1[g] = lcol[...]

    def ar(hh):
        return rcopy(rcol, right.at[slot], sem_sr.at[hh], sem_rr.at[slot], g * XC + xc_d, hh)

    for hh in range(H):
        here = own_writer & (h == hh)

        @pl.when(jnp.logical_not(here))
        def _():
            ar(hh).start()

        @pl.when(here)
        def _():
            right[slot] = rcol[...]

    def aa1(o):
        t = (xc + o) % XC
        rows = pl.ds(pl.multiple_of(t * G, G), G)
        return rcopy(acol.at[rows], ra1.at[xc], sem_sa1.at[t], sem_ra1.at[xc], dxc(o), h)

    each(XC, lambda o: aa1(o).start())
    ra1[xc] = acol[pl.ds(pl.multiple_of(xc * G, G), G), :]

    def wait_l1(o):
        gg = (g + o) % G
        rcopy(lcol, l1.at[gg], sem_sl1.at[gg], sem_rl1.at[gg], dg(o), h).wait_recv()

    each(G, wait_l1)
    tmpl[...] = l1[...].astype(F32).reshape(G * CC, S)
    own_rows = pl.ds(pl.multiple_of(core * X * G + xx * G, G), G)
    for c in range(CC):
        left[c, own_rows, :] = tmpl[pl.ds(c, G, stride=CC), :].astype(BF)

    def al2(o):
        t = (xx + o) % X
        dst = left.at[:, own_rows, :]
        return rcopy(dst, dst, sem_sl2.at[t], sem_rl2.at[xx], g * XC + 2 * t + core, h)

    each(X, lambda o: al2(o).start())

    def wait_a1(o):
        t = (xc + o) % XC
        rows = pl.ds(pl.multiple_of(t * G, G), G)
        rcopy(acol.at[rows], ra1.at[t], sem_sa1.at[t], sem_ra1.at[t], dxc(o), h).wait_recv()

    each(XC, wait_a1)
    swap(ra1, tmpa, sa2)

    def aa2(o):
        gg = (g + o) % G
        return rcopy(sa2.at[gg], o0_ref.at[g, h], sem_sa2.at[gg], sem_ra2.at[g], dg(o), h)

    each(G, lambda o: aa2(o).start())
    o0_ref[g, h] = sa2[g]

    for k in range(H):
        ms = H * xc + k
        src_h, src_xc = ms // XC, ms % XC

        @pl.when(jnp.logical_not((src_h == h) & (src_xc == xc)))
        def _():
            rcopy(rcol, right.at[k], sem_sr.at[0], sem_rr.at[k], g * XC + src_xc, src_h).wait_recv()

    for k in range(H):
        rk = right[k].astype(F32).T.astype(BF)
        for c in range(CC):
            z[c * S : (c + 1) * S, k * CZ : (k + 1) * CZ] = jnp.dot(
                rk, pw_ref[c * CC : (c + 1) * CC, :], preferred_element_type=F32
            ).astype(BF)

    def wait_l2(o):
        t = (xx + o) % X
        dst = left.at[:, pl.ds(pl.multiple_of(core * X * G + t * G, G), G), :]
        rcopy(dst, dst, sem_sl2.at[t], sem_rl2.at[t], g * XC + 2 * t + core, h).wait_recv()

    each(X, wait_l2)
    sib = g * XC + 2 * xx + (1 - core)
    mine = left.at[:, pl.ds(pl.multiple_of(core * X * G, X * G), X * G), :]
    theirs = left.at[:, pl.ds(pl.multiple_of((1 - core) * X * G, X * G), X * G), :]
    al3 = rcopy(mine, mine, sem_sl3, sem_rl3, sib, h)
    al3.start()

    def wait_a2(o):
        gg = (g + o) % G
        rcopy(sa2.at[gg], o0_ref.at[gg, h], sem_sa2.at[gg], sem_ra2.at[gg], dg(o), h).wait_recv()

    each(G, wait_a2)

    def aa3(o):
        hh = (h + o) % H
        return rcopy(o0_ref.at[:, h], o0_ref.at[:, h], sem_sa3.at[hh], sem_ra3.at[h], d, hh)

    each(H, lambda o: aa3(o).start())

    rcopy(theirs, theirs, sem_sl3, sem_rl3, sib, h).wait_recv()
    rows = jnp.concatenate([left[c] for c in range(CC)], axis=1)
    total = jnp.dot(rows, z[...], preferred_element_type=F32) * (1.0 / S)
    total = total + jnp.concatenate([bias_ref[...]] * H, axis=1)
    for hh in range(H):
        res[hh] = jnp.concatenate(
            [total[:, k * CZ + hh * ZQ : k * CZ + (hh + 1) * ZQ] for k in range(H)], axis=1
        ).astype(BF)

    def ax(o):
        hh = (h + o) % H
        return rcopy(res.at[hh], o1_ref.at[h], sem_sx.at[hh], sem_rx.at[h], d, hh)

    each(H, lambda o: ax(o).start())
    o1_ref[h] = res[h]

    def wait_x(o):
        hh = (h + o) % H
        rcopy(res.at[hh], o1_ref.at[hh], sem_sx.at[hh], sem_rx.at[hh], d, hh).wait_recv()

    each(H, wait_x)

    def wait_a3(o):
        hh = (h + o) % H
        rcopy(o0_ref.at[:, hh], o0_ref.at[:, hh], sem_sa3.at[hh], sem_ra3.at[hh], d, hh).wait_recv()

    each(H, wait_a3)
    each(G, lambda o: a1(o).wait_send())
    each(H, lambda o: aw(o).wait_send())
    each(XC, lambda o: a2(o).wait_send())
    each(G, lambda o: al1(o).wait_send())
    for hh in range(H):

        @pl.when(jnp.logical_not(own_writer & (h == hh)))
        def _():
            ar(hh).wait_send()

    each(XC, lambda o: aa1(o).wait_send())
    each(X, lambda o: al2(o).wait_send())
    each(G, lambda o: aa2(o).wait_send())
    al3.wait_send()
    each(H, lambda o: aa3(o).wait_send())
    each(H, lambda o: ax(o).wait_send())


def shards(mesh, x, gain1, wq, wk, wv, wg, wo, gain2, f1, f2, pw, bias):
    D, H = mesh.shape["dap"], mesh.shape["head"]
    G, X = D // XC, XC // 2
    S = D
    CM = x.shape[2]
    HW, FC, CC, CZ = wq.shape[1], f1.shape[1], f2.shape[1], pw.shape[1]
    vm = pl.BlockSpec(memory_space=pltpu.VMEM)
    dma = pltpu.SemaphoreType.DMA
    scratch = [
        pltpu.VMEM((4 * HW + 16, CM), BF),
        pltpu.VMEM((H, 4 * HW + 16, CM), BF),
        pltpu.VMEM((CC, CM), BF),
        pltpu.VMEM((G, XC, CM), BF),
        pltpu.VMEM((CM // 128, S, 128), F32),
        pltpu.VMEM((XC, G, CM), BF),
        pltpu.VMEM((S, CM), BF),
        pltpu.VMEM((S, CM), BF),
        pltpu.VMEM((CC, S), BF),
        pltpu.VMEM((CC, S), BF),
        pltpu.VMEM((G, CC, S), BF),
        pltpu.VMEM((G * CC, S), F32),
        pltpu.VMEM((CC, S, S), BF),
        pltpu.VMEM((H, CC, S), BF),
        pltpu.VMEM((CC * S, H * CZ), BF),
        pltpu.VMEM((H, S, CZ), BF),
        pltpu.VMEM((XC, G, CM), BF),
        pltpu.VMEM((CM // 128, S, 128), F32),
        pltpu.VMEM((G, XC, CM), BF),
    ]
    sems = [G, G, H, H, XC, XC, G, G, X, X, None, None, H, H, XC, XC, G, G, H, H, H, H, 2]
    scratch += [dma if n is None else dma((n,)) for n in sems]
    o0, o1 = pl.pallas_call(
        functools.partial(kernel, (G, H, CM)),
        out_shape=(
            jax.ShapeDtypeStruct((G, H, XC, CM), BF),
            jax.ShapeDtypeStruct((H, S, CZ), BF),
        ),
        in_specs=[pl.BlockSpec(memory_space=pl.ANY)] + [vm] * 11,
        out_specs=(vm, vm),
        scratch_shapes=scratch,
        compiler_params=pltpu.CompilerParams(
            collective_id=0, has_side_effects=True, vmem_limit_bytes=40 * 1024 * 1024
        ),
    )(
        x.reshape(G, H, XC, CM), wq, wk, wv, wg, wo, gain1.reshape(1, CM), gain2.reshape(1, CM), f1, f2, pw,
        bias.reshape(1, CZ),
    )
    after = o0.reshape(1, G * H * XC, CM)
    delta = o1.reshape(H, 2, X, G, H, CZ // H).transpose(3, 0, 2, 1, 4, 5)
    return after, delta.reshape(G * H * XC, H, CZ // H)


def solution(mesh):
    placed = (
        P("dap", None, None),
        P(),
        P(None, "head"),
        P(None, "head"),
        P(None, "head"),
        P(None, "head"),
        P(),
        P(),
        P(None, "head"),
        P(),
        P(),
        P(),
    )
    return jax.shard_map(
        functools.partial(shards, mesh),
        mesh=mesh,
        in_specs=placed,
        out_specs=(P("dap", None, None), P(None, "dap", "head")),
        check_vma=False,
    )
```

time: 232 us -> 66.5 us (0.29)
  waiting for transfers between devices: 139 us -> 0 us
  Pallas kernels: 0 us -> 57.4 us
  blocking collectives: 32.4 us -> 0 us
  starting transfers between devices: 30 us -> 0 us
  between operations: 14.3 us -> 0.75 us
  matrix products: 8.24 us -> 0 us
  local copies, waits for them, and re-layouts: 4.93 us -> 7.58 us
    all_gather x1 -> x0, waiting for transfers between devices: 83.6 us -> none  [shards(): lax.all_gather(first_factor, 'dap', axis=0, tiled=True)]
    pallas_call x0 -> x1, Pallas kernels: none -> 57.4 us  [shards(): pl.pallas_call(functools.partial(kernel, (G, H, CM)), out_shape=(jax.Shap...]
    all_to_all x2 -> x0, waiting for transfers between devices: 32.4 us -> none  [the longest x1 16.3 us: shards(): lax.all_to_all(second_factor, 'dap', split_axis=1, concat_axis=0, tiled=T...]
    all_to_all x2 -> x0, starting transfers between devices: 29.9 us -> none  [the longest x1 20.9 us: shards(): lax.all_to_all(stacked_tensor, 'dap', split_axis=1, concat_axis=0, tiled=...]
    reduce_scatter x1 -> x0, waiting for transfers between devices: 22.9 us -> none  [shards(): lax.psum_scatter(partial_value.astype(jnp.bfloat16), 'head', scatter_dime...]
    all_to_all x1 -> x0, blocking collectives: 21.4 us -> none  [back_rows(): return lax.all_to_all(mixed, 'dap', split_axis=0, concat_axis=1, tiled=True)]
    all_gather x1 -> x0, blocking collectives: 11 us -> none  [shards(): lax.all_gather(flat, 'head', axis=2, tiled=True)]
    dot_general x17 -> x0, matrix products: 7.14 us -> none  [the longest x1 2.12 us: shards(): jnp.einsum('sic,sje->ijce', lax.all_gather(first_factor, 'dap', axis=0, t...]
  transfers between devices with their start and end apart: 4 -> 0, of which waited for: 4 -> 0; matrix products, arithmetic and copies ran while one was open for 1% -> 0% of each run, Pallas kernels for 0% -> 0%
where the time goes in v1:
time: 66.5 us; the launch traced here: 65.7 us
  Pallas kernels  57.4 us (86%)
  local copies, waits for them, and re-layouts  7.58 us (11%)
  between operations  0.75 us (1%)
    pallas_call x1, Pallas kernels, shards(): pl.pallas_call(functools.partial(kernel, (G, H, CM)), out_shape=(jax.Shap...  57.4 us
    unnamed x24, local copies, waits for them, and re-layouts  6.81 us

profile of v1, /device:TPU:1, one launch (start us, length us, event | category | flops | bytes accessed | tf_op | source)
XLA Modules:
  0.0 65.7 jit_solution(6992255318209286508)
XLA Ops:
  0.6 0.0 copy-start.7
  0.6 0.0 copy-start.6
  0.7 0.0 copy-start
  0.7 0.0 copy-start.1
  0.7 0.9 %copy.21.wq_ref = bf16[256,64]{1,0:T(8,128)(2,1)S(1)} copy(bf16[256,64]{0,1:T(8,128)(2,1)} %param.14) | data formatting | bytes 65536 | tf_op args[2]
  1.6 0.9 %copy.22.wk_ref = bf16[256,64]{1,0:T(8,128)(2,1)S(1)} copy(bf16[256,64]{0,1:T(8,128)(2,1)} %param.15) | data formatting | bytes 65536 | tf_op args[3]
  2.5 0.9 %copy.23.wv_ref = bf16[256,64]{1,0:T(8,128)(2,1)S(1)} copy(bf16[256,64]{0,1:T(8,128)(2,1)} %param.16) | data formatting | bytes 65536 | tf_op args[4]
  3.4 0.9 %copy.24.wg_ref = bf16[256,64]{1,0:T(8,128)(2,1)S(1)} copy(bf16[256,64]{0,1:T(8,128)(2,1)} %param.17) | data formatting | bytes 65536 | tf_op args[5]
  4.2 0.0 copy-done.7
  4.3 0.1 copy.25.f1_ref
  4.4 0.0 copy-done.6
  4.4 0.0 copy-start.3
  4.4 0.0 copy-start.4
  4.4 0.0 copy-start.5
  4.4 0.1 copy.26.f2_ref
  4.5 0.0 copy-done
  4.6 0.5 copy-done.3
  5.1 0.0 copy-done.4
  5.1 0.9 %copy-done.2 = bf16[256,256]{1,0:T(8,128)(2,1)S(1)} copy-done((bf16[256,256]{1,0:T(8,128)(2,1)S(1)}, bf16[256,256]{1,0:T(8,128)(2,1)}, u32[]{:S(2)}) %copy-start.2) | copy-done | bytes 131096
  6.0 57.4 %shard_map.131 = (bf16[16,4,8,256]{3,2,1,0:T(8,128)(2,1)S(1)}, bf16[4,128,128]{2,1,0:T(8,128)(2,1)S(1)}) custom-call(bf16[16,4,8,256]{3,2,1,0:T(8,128)(2,1)S(1)} %bitcast.9, bf16[256,64]{1,0:T(8,128)(2,1)S(1)} %copy.21.wq_ref, bf16[256,64]{1,0:T(8,128)(2,1)S(1)} %copy.22.wk_ref, bf16[256,64]{1,0:T(8,128)(2,1)S(1)} %copy.23.wv_ref, ...), custom_call_target="tpu_custom_call" | custom-call | tf_op jit(solution)/shard_map/pallas_call | solution.py:355
  63.4 0.2 reshape.30
  63.6 0.5 copy.27
  64.2 0.8 %copy.28 = bf16[512,4,32]{0,2,1:T(8,128)(2,1)} copy(bf16[512,4,32]{2,0,1:T(8,128)(2,1)S(1)} %bitcast.13) | data formatting | bytes 262144
  65.0 0.7 %copy.30 = bf16[1,512,256]{2,1,0:T(8,128)(2,1)} copy(bf16[1,512,256]{2,1,0:T(8,128)(2,1)S(1)} %bitcast.8) | data formatting | bytes 524288
  (3 shorter events, 0.0 us)
Async XLA Ops:
  0.6 3.6 %copy-start.7 = (bf16[256,8]{0,1:T(8,128)(2,1)S(1)}, bf16[256,8]{0,1:T(8,128)(2,1)}, u32[]{:S(2)}) copy-start(bf16[256,8]{0,1:T(8,128)(2,1)} %param.20) | copy-start | bytes 12292
  0.6 3.7 %copy-start.6 = (bf16[256,32]{0,1:T(8,128)(2,1)S(1)}, bf16[256,32]{0,1:T(8,128)(2,1)}, u32[]{:S(2)}) copy-start(bf16[256,32]{0,1:T(8,128)(2,1)} %param.21) | copy-start | bytes 49156
  0.7 3.9 %copy-start = (bf16[1,512,256]{2,1,0:T(8,128)(2,1)S(1)}, bf16[1,512,256]{2,1,0:T(8,128)(2,1)}, u32[]{:S(2)}) copy-start(bf16[1,512,256]{2,1,0:T(8,128)(2,1)} %param.12) | copy-start | bytes 786436
  0.7 3.9 %copy-start.1 = (bf16[1024,128]{1,0:T(8,128)(2,1)S(1)}, bf16[1024,128]{1,0:T(8,128)(2,1)}, u32[]{:S(2)}) copy-start(bf16[1024,128]{1,0:T(8,128)(2,1)} %pw_ref.1) | copy-start | bytes 786436
  4.4 0.7 %copy-start.3 = (f32[256]{0:T(256)S(1)}, f32[256]{0:T(256)}, u32[]{:S(2)}) copy-start(f32[256]{0:T(256)} %param.13) | copy-start | bytes 3076
  4.4 0.7 %copy-start.4 = (f32[256]{0:T(256)S(1)}, f32[256]{0:T(256)}, u32[]{:S(2)}) copy-start(f32[256]{0:T(256)} %param.19) | copy-start | bytes 3076
  4.4 0.7 %copy-start.5 = (f32[128]{0:T(128)S(1)}, f32[128]{0:T(128)}, u32[]{:S(2)}) copy-start(f32[128]{0:T(128)} %param.23) | copy-start | bytes 1540
  5.1 0.9 %copy-start.2 = (bf16[256,256]{1,0:T(8,128)(2,1)S(1)}, bf16[256,256]{1,0:T(8,128)(2,1)}, u32[]{:S(2)}) copy-start(bf16[256,256]{1,0:T(8,128)(2,1)} %wo_ref.1) | copy-start | bytes 393220

commit v2 on v1

--- a/solution.py
+++ b/solution.py
@@ -37,20 +37,22 @@
 
 def kernel(
     dims,
-    x_ref, wq_ref, wk_ref, wv_ref, wg_ref, wo_ref, gain1_ref, gain2_ref, f1_ref, f2_ref, pw_ref, bias_ref,
+    x_hbm, wq_hbm, wk_hbm, wv_hbm, wg_hbm, wo_hbm, gain1_hbm, gain2_hbm, f1_hbm, f2_hbm, pw_hbm, bias_hbm,
     o0_ref, o1_ref,
-    wsend, wall, s2t, r1, tmp, s2, r2, acol, lcol, rcol, l1, tmpl, left, right, z, res, ra1, tmpa, sa2,
+    wsend, wall, wo_ref, gain1_ref, gain2_ref, f1_ref, f2_ref, pw_ref, bias_ref, bias_t, place,
+    r1, tmp, s2, r2, acol, lcol, rcol, l1, tmpl, left, right, z, res, rx, ra1, tmpa, sa2,
     sem_s1, sem_r1, sem_sw, sem_rw, sem_s2, sem_r2, sem_sl1, sem_rl1, sem_sl2, sem_rl2, sem_sl3, sem_rl3,
-    sem_sr, sem_rr, sem_sa1, sem_ra1, sem_sa2, sem_ra2, sem_sa3, sem_ra3, sem_sx, sem_rx, sem_loc,
+    sem_sr, sem_rr, sem_sa1, sem_ra1, sem_sa2, sem_ra2, sem_sa3, sem_ra3, sem_sx, sem_rx, sem_loc, sem_in,
 ):
     G, H, CM = dims
     X = XC // 2
     S = G * XC
-    HW = wq_ref.shape[1]
+    N = S * H
+    HW = wq_hbm.shape[0]
     NH = HW // HEAD_DIMENSION
-    FC = f1_ref.shape[1]
-    CC = f2_ref.shape[1]
-    CZ = pw_ref.shape[1]
+    FC = f1_hbm.shape[0]
+    CC = f2_hbm.shape[0]
+    CZ = pw_hbm.shape[1]
     ZQ = CZ // H
     d = lax.axis_index("dap")
     h = lax.axis_index("head")
@@ -98,21 +100,32 @@
         def _():
             signal(g * XC + src_xc, src_h)
 
-    for i, w in enumerate((wq_ref, wk_ref, wv_ref, wg_ref)):
-        wsend[i * HW : (i + 1) * HW, :] = w[...].astype(F32).T.astype(BF)
-    f1t = jnp.concatenate([f1_ref[...].astype(F32), jnp.zeros((CM, 128 - FC), F32)], axis=1).T
-    wsend[4 * HW :, :] = f1t[:16].astype(BF)
-    s2t[...] = jnp.concatenate([f2_ref[...].astype(F32), jnp.zeros((CM, 128 - CC), F32)], axis=1).T[:CC].astype(BF)
+    ins = [
+        pltpu.make_async_copy(w, wsend.at[pl.ds(i * HW, HW)], sem_in.at[i])
+        for i, w in enumerate((wq_hbm, wk_hbm, wv_hbm, wg_hbm))
+    ]
+    for w, ref in (
+        (f1_hbm, f1_ref), (f2_hbm, f2_ref), (gain1_hbm, gain1_ref), (gain2_hbm, gain2_ref), (wo_hbm, wo_ref),
+        (bias_hbm, bias_ref), (pw_hbm, pw_ref),
+    ):
+        ins.append(pltpu.make_async_copy(w, ref, sem_in.at[len(ins)]))
+    for copy in ins:
+        copy.start()
+    loc1 = pltpu.make_async_copy(x_hbm.at[g, h], r1.at[g], sem_loc.at[0])
+    loc1.start()
+    for copy in ins[:5]:
+        copy.wait()
+    wsend[4 * HW :, :] = jnp.concatenate(
+        [f1_ref[...].astype(F32), jnp.zeros((16 - FC, CM), F32)], axis=0
+    ).astype(BF) if FC < 16 else f1_ref[...]
 
     pl.semaphore_wait(barrier, (G - 1) + (XC - 1) + (H - 1) + H - jnp.where(own_writer, 1, 0))
 
     def a1(o):
         gg = (g + o) % G
-        return rcopy(x_ref.at[gg, h], r1.at[g], sem_s1.at[gg], sem_r1.at[g], dg(o), h)
+        return rcopy(x_hbm.at[gg, h], r1.at[g], sem_s1.at[gg], sem_r1.at[g], dg(o), h)
 
     each(G, lambda o: a1(o).start())
-    loc1 = pltpu.make_async_copy(x_ref.at[g, h], r1.at[g], sem_loc.at[0])
-    loc1.start()
 
     def aw(o):
         hh = (h + o) % H
@@ -122,9 +135,16 @@
     loc2 = pltpu.make_async_copy(wsend, wall.at[h], sem_loc.at[1])
     loc2.start()
 
+    for copy in ins[5:]:
+        copy.wait()
+    bias_t[...] = jnp.broadcast_to(bias_ref[...], (CZ, CZ)).T[:, :1] + jnp.zeros((CZ, S), F32)
+    row = lax.broadcasted_iota(jnp.int32, (N, 1), 0)
+    at = (row % G) * (H * XC) + (row // S) * XC + ((row // G) % X) * 2 + (row // (X * G)) % 2
+    place[...] = jnp.where(lax.broadcasted_iota(jnp.int32, (N, N), 1) == at, 1.0, 0.0).astype(BF)
+
     def wait_r1(o):
         gg = (g + o) % G
-        rcopy(x_ref.at[gg, h], r1.at[gg], sem_s1.at[gg], sem_r1.at[gg], dg(o), h).wait_recv()
+        rcopy(x_hbm.at[gg, h], r1.at[gg], sem_s1.at[gg], sem_r1.at[gg], dg(o), h).wait_recv()
 
     loc1.wait()
     each(G, wait_r1)
@@ -174,7 +194,7 @@
     normed2 = standardize(after.astype(F32), gain2_ref[...])
     f1 = jnp.concatenate([wall[hp, 4 * HW :, :].astype(F32)[:FC] for hp in range(H)], axis=0).astype(BF)
     lcol[...] = dot(f1, normed2, 1, 1).astype(BF)
-    rcol[...] = dot(s2t[...], normed2, 1, 1).astype(BF)
+    rcol[...] = dot(f2_ref[...], normed2, 1, 1).astype(BF)
 
     def al1(o):
         gg = (g + o) % G
@@ -245,12 +265,11 @@
         def _():
             rcopy(rcol, right.at[k], sem_sr.at[0], sem_rr.at[k], g * XC + src_xc, src_h).wait_recv()
 
-    for k in range(H):
-        rk = right[k].astype(F32).T.astype(BF)
-        for c in range(CC):
-            z[c * S : (c + 1) * S, k * CZ : (k + 1) * CZ] = jnp.dot(
-                rk, pw_ref[c * CC : (c + 1) * CC, :], preferred_element_type=F32
-            ).astype(BF)
+    rights = jnp.concatenate([right[k] for k in range(H)], axis=1)
+    for c in range(CC):
+        zc = dot(pw_ref[c * CC : (c + 1) * CC, :], rights, 0, 0).astype(BF)
+        for k in range(H):
+            z[k * CZ : (k + 1) * CZ, c * S : (c + 1) * S] = zc[:, k * S : (k + 1) * S]
 
     def wait_l2(o):
         t = (xx + o) % X
@@ -278,25 +297,28 @@
 
     rcopy(theirs, theirs, sem_sl3, sem_rl3, sib, h).wait_recv()
     rows = jnp.concatenate([left[c] for c in range(CC)], axis=1)
-    total = jnp.dot(rows, z[...], preferred_element_type=F32) * (1.0 / S)
-    total = total + jnp.concatenate([bias_ref[...]] * H, axis=1)
+    total = dot(z[...], rows, 1, 1) * (1.0 / S)
     for hh in range(H):
-        res[hh] = jnp.concatenate(
-            [total[:, k * CZ + hh * ZQ : k * CZ + (hh + 1) * ZQ] for k in range(H)], axis=1
-        ).astype(BF)
+        for k in range(H):
+            res[hh, k * ZQ : (k + 1) * ZQ, :] = (
+                total[k * CZ + hh * ZQ : k * CZ + (hh + 1) * ZQ] + bias_t[hh * ZQ : (hh + 1) * ZQ]
+            ).astype(BF)
 
     def ax(o):
         hh = (h + o) % H
-        return rcopy(res.at[hh], o1_ref.at[h], sem_sx.at[hh], sem_rx.at[h], d, hh)
+        return rcopy(res.at[hh], rx.at[h], sem_sx.at[hh], sem_rx.at[h], d, hh)
 
     each(H, lambda o: ax(o).start())
-    o1_ref[h] = res[h]
+    rx[h] = res[h]
 
     def wait_x(o):
         hh = (h + o) % H
-        rcopy(res.at[hh], o1_ref.at[hh], sem_sx.at[hh], sem_rx.at[hh], d, hh).wait_recv()
+        rcopy(res.at[hh], rx.at[hh], sem_sx.at[hh], sem_rx.at[hh], d, hh).wait_recv()
 
     each(H, wait_x)
+    o1_ref[...] = jnp.dot(
+        jnp.concatenate([rx[k] for k in range(H)], axis=1), place[...], preferred_element_type=F32
+    ).astype(BF)
 
     def wait_a3(o):
         hh = (h + o) % H
@@ -328,11 +350,20 @@
     CM = x.shape[2]
     HW, FC, CC, CZ = wq.shape[1], f1.shape[1], f2.shape[1], pw.shape[1]
     vm = pl.BlockSpec(memory_space=pltpu.VMEM)
+    hbm = pl.BlockSpec(memory_space=pltpu.HBM)
     dma = pltpu.SemaphoreType.DMA
     scratch = [
         pltpu.VMEM((4 * HW + 16, CM), BF),
         pltpu.VMEM((H, 4 * HW + 16, CM), BF),
+        pltpu.VMEM((CM, CM), BF),
+        pltpu.VMEM((1, CM), F32),
+        pltpu.VMEM((1, CM), F32),
+        pltpu.VMEM((FC, CM), BF),
         pltpu.VMEM((CC, CM), BF),
+        pltpu.VMEM((CC * CC, CZ), BF),
+        pltpu.VMEM((1, CZ), F32),
+        pltpu.VMEM((CZ, S), F32),
+        pltpu.VMEM((S * H, S * H), BF),
         pltpu.VMEM((G, XC, CM), BF),
         pltpu.VMEM((CM // 128, S, 128), F32),
         pltpu.VMEM((XC, G, CM), BF),
@@ -344,33 +375,32 @@
         pltpu.VMEM((G * CC, S), F32),
         pltpu.VMEM((CC, S, S), BF),
         pltpu.VMEM((H, CC, S), BF),
-        pltpu.VMEM((CC * S, H * CZ), BF),
-        pltpu.VMEM((H, S, CZ), BF),
+        pltpu.VMEM((H * CZ, CC * S), BF),
+        pltpu.VMEM((H, CZ, S), BF),
+        pltpu.VMEM((H, CZ, S), BF),
         pltpu.VMEM((XC, G, CM), BF),
         pltpu.VMEM((CM // 128, S, 128), F32),
         pltpu.VMEM((G, XC, CM), BF),
     ]
-    sems = [G, G, H, H, XC, XC, G, G, X, X, None, None, H, H, XC, XC, G, G, H, H, H, H, 2]
+    sems = [G, G, H, H, XC, XC, G, G, X, X, None, None, H, H, XC, XC, G, G, H, H, H, H, 2, 11]
     scratch += [dma if n is None else dma((n,)) for n in sems]
     o0, o1 = pl.pallas_call(
         functools.partial(kernel, (G, H, CM)),
         out_shape=(
             jax.ShapeDtypeStruct((G, H, XC, CM), BF),
-            jax.ShapeDtypeStruct((H, S, CZ), BF),
+            jax.ShapeDtypeStruct((CZ, H * S), BF),
         ),
-        in_specs=[pl.BlockSpec(memory_space=pl.ANY)] + [vm] * 11,
+        in_specs=[hbm] * 12,
         out_specs=(vm, vm),
         scratch_shapes=scratch,
         compiler_params=pltpu.CompilerParams(
             collective_id=0, has_side_effects=True, vmem_limit_bytes=40 * 1024 * 1024
         ),
     )(
-        x.reshape(G, H, XC, CM), wq, wk, wv, wg, wo, gain1.reshape(1, CM), gain2.reshape(1, CM), f1, f2, pw,
-        bias.reshape(1, CZ),
+        x.reshape(G, H, XC, CM), wq.T, wk.T, wv.T, wg.T, wo, gain1.reshape(1, CM), gain2.reshape(1, CM), f1.T, f2.T,
+        pw, bias.reshape(1, CZ),
     )
-    after = o0.reshape(1, G * H * XC, CM)
-    delta = o1.reshape(H, 2, X, G, H, CZ // H).transpose(3, 0, 2, 1, 4, 5)
-    return after, delta.reshape(G * H * XC, H, CZ // H)
+    return o0.reshape(1, G * H * XC, CM), o1.reshape(H, CZ // H, H * S).transpose(2, 0, 1)
 
 
 def solution(mesh):

time: 66.5 us -> 68.2 us (1.026)
  Pallas kernels: 57.4 us -> 58.4 us
  local copies, waits for them, and re-layouts: 7.58 us -> 8.57 us
    unnamed x24 -> x26, local copies, waits for them, and re-layouts: 6.81 us -> 8.57 us
    pallas_call x1, Pallas kernels: 57.4 us -> 58.4 us  [shards(): pl.pallas_call(functools.partial(kernel, (G, H, CM)), out_shape=(jax.Shap...]
    reshape x2 -> x0, local copies, waits for them, and re-layouts: 0.78 us -> none  [shards(): delta = o1.reshape(H, 2, X, G, H, CZ // H).transpose(3, 0, 2, 1, 4, 5)]
where the time goes in v2:
time: 68.2 us; the launch traced here: 67.7 us
  Pallas kernels  58.4 us (86%)
  local copies, waits for them, and re-layouts  8.57 us (13%)
  between operations  0.69 us (1%)
    pallas_call x1, Pallas kernels, shards(): pl.pallas_call(functools.partial(kernel, (G, H, CM)), out_shape=(jax.Shap...  58.4 us
    unnamed x26, local copies, waits for them, and re-layouts  8.57 us

profile of v2, /device:TPU:1, one launch (start us, length us, event | category | flops | bytes accessed | tf_op | source)
XLA Modules:
  0.0 67.7 jit_solution(8581614254536085998)
XLA Ops:
  0.6 0.0 copy-start.7
  0.6 0.0 copy-start.10
  0.7 0.0 copy-start.9
  0.7 0.0 copy-start.11
  0.7 0.7 %copy-done.7 = bf16[256,32]{0,1:T(8,128)(2,1)S(1)} copy-done((bf16[256,32]{0,1:T(8,128)(2,1)S(1)}, bf16[256,32]{0,1:T(8,128)(2,1)}, u32[]{:S(2)}) %copy-start.7) | copy-done | bytes 16408
  1.4 0.0 copy-done.10
  1.4 0.0 copy-done.9
  1.4 0.0 copy-done.11
  1.4 0.0 copy-start
  1.4 0.9 %copy-done = bf16[1,512,256]{2,1,0:T(8,128)(2,1)S(1)} copy-done((bf16[1,512,256]{2,1,0:T(8,128)(2,1)S(1)}, bf16[1,512,256]{2,1,0:T(8,128)(2,1)}, u32[]{:S(2)}) %copy-start) | copy-done | bytes 262168
  2.3 0.0 copy-start.1
  2.3 0.9 %copy-done.1 = bf16[1024,128]{1,0:T(8,128)(2,1)S(1)} copy-done((bf16[1024,128]{1,0:T(8,128)(2,1)S(1)}, bf16[1024,128]{1,0:T(8,128)(2,1)}, u32[]{:S(2)}) %copy-start.1) | copy-done | bytes 262168
  3.3 0.0 copy-start.2
  3.3 0.9 %copy-done.2 = bf16[256,256]{1,0:T(8,128)(2,1)S(1)} copy-done((bf16[256,256]{1,0:T(8,128)(2,1)S(1)}, bf16[256,256]{1,0:T(8,128)(2,1)}, u32[]{:S(2)}) %copy-start.2) | copy-done | bytes 131096
  4.2 0.0 copy-start.3
  4.2 0.8 %copy-done.3 = bf16[256,64]{0,1:T(8,128)(2,1)S(1)} copy-done((bf16[256,64]{0,1:T(8,128)(2,1)S(1)}, bf16[256,64]{0,1:T(8,128)(2,1)}, u32[]{:S(2)}) %copy-start.3) | copy-done | bytes 32792
  4.9 0.0 copy-start.4
  4.9 0.8 %copy-done.4 = bf16[256,64]{0,1:T(8,128)(2,1)S(1)} copy-done((bf16[256,64]{0,1:T(8,128)(2,1)S(1)}, bf16[256,64]{0,1:T(8,128)(2,1)}, u32[]{:S(2)}) %copy-start.4) | copy-done | bytes 32792
  5.7 0.8 %copy-done.5 = bf16[256,64]{0,1:T(8,128)(2,1)S(1)} copy-done((bf16[256,64]{0,1:T(8,128)(2,1)S(1)}, bf16[256,64]{0,1:T(8,128)(2,1)}, u32[]{:S(2)}) %copy-start.5) | copy-done | bytes 32792
  6.4 0.8 %copy-done.6 = bf16[256,64]{0,1:T(8,128)(2,1)S(1)} copy-done((bf16[256,64]{0,1:T(8,128)(2,1)S(1)}, bf16[256,64]{0,1:T(8,128)(2,1)}, u32[]{:S(2)}) %copy-start.6) | copy-done | bytes 32792
  7.2 0.7 %copy-done.8 = bf16[256,8]{0,1:T(8,128)(2,1)S(1)} copy-done((bf16[256,8]{0,1:T(8,128)(2,1)S(1)}, bf16[256,8]{0,1:T(8,128)(2,1)}, u32[]{:S(2)}) %copy-start.8) | copy-done | bytes 4120
  7.9 58.4 %shard_map.131 = (bf16[16,4,8,256]{3,2,1,0:T(8,128)(2,1)S(1)}, bf16[128,512]{1,0:T(8,128)(2,1)S(1)}) custom-call(bf16[16,4,8,256]{3,2,1,0:T(8,128)(2,1)S(1)} %bitcast.15, bf16[64,256]{1,0:T(8,128)(2,1)S(1)} %bitcast.17, bf16[64,256]{1,0:T(8,128)(2,1)S(1)} %bitcast.18, bf16[64,256]{1,0:T(8,128)(2,1)S(1)} %bitcast.19, bf16[64,256]{1,0:T(8,128)(2,1)S(1)} %bitcast.20, ...), custom_call_target="tpu_custom_call" | custom-call | tf_op jit(solution)/shard_map/pallas_call | solution.py:387
  66.3 0.7 %copy.16 = bf16[1,512,256]{2,1,0:T(8,128)(2,1)} copy(bf16[1,512,256]{2,1,0:T(8,128)(2,1)S(1)} %bitcast.14) | data formatting | bytes 524288
  67.0 0.7 copy.17
  (3 shorter events, 0.0 us)
Async XLA Ops:
  0.6 0.7 %copy-start.7 = (bf16[256,32]{0,1:T(8,128)(2,1)S(1)}, bf16[256,32]{0,1:T(8,128)(2,1)}, u32[]{:S(2)}) copy-start(bf16[256,32]{0,1:T(8,128)(2,1)} %param.21) | copy-start | bytes 49156
  0.6 0.7 %copy-start.10 = (f32[256]{0:T(256)S(1)}, f32[256]{0:T(256)}, u32[]{:S(2)}) copy-start(f32[256]{0:T(256)} %param.19) | copy-start | bytes 3076
  0.7 0.7 %copy-start.9 = (f32[256]{0:T(256)S(1)}, f32[256]{0:T(256)}, u32[]{:S(2)}) copy-start(f32[256]{0:T(256)} %param.13) | copy-start | bytes 3076
  0.7 0.7 %copy-start.11 = (f32[128]{0:T(128)S(1)}, f32[128]{0:T(128)}, u32[]{:S(2)}) copy-start(f32[128]{0:T(128)} %param.23) | copy-start | bytes 1540
  1.4 1.0 %copy-start = (bf16[1,512,256]{2,1,0:T(8,128)(2,1)S(1)}, bf16[1,512,256]{2,1,0:T(8,128)(2,1)}, u32[]{:S(2)}) copy-start(bf16[1,512,256]{2,1,0:T(8,128)(2,1)} %param.12) | copy-start | bytes 786436
  2.3 0.9 %copy-start.1 = (bf16[1024,128]{1,0:T(8,128)(2,1)S(1)}, bf16[1024,128]{1,0:T(8,128)(2,1)}, u32[]{:S(2)}) copy-start(bf16[1024,128]{1,0:T(8,128)(2,1)} %pw_hbm.1) | copy-start | bytes 786436
  3.3 0.9 %copy-start.2 = (bf16[256,256]{1,0:T(8,128)(2,1)S(1)}, bf16[256,256]{1,0:T(8,128)(2,1)}, u32[]{:S(2)}) copy-start(bf16[256,256]{1,0:T(8,128)(2,1)} %wo_hbm.1) | copy-start | bytes 393220
  4.2 0.8 %copy-start.3 = (bf16[256,64]{0,1:T(8,128)(2,1)S(1)}, bf16[256,64]{0,1:T(8,128)(2,1)}, u32[]{:S(2)}) copy-start(bf16[256,64]{0,1:T(8,128)(2,1)} %param.14) | copy-start | bytes 98308
  4.9 0.8 %copy-start.4 = (bf16[256,64]{0,1:T(8,128)(2,1)S(1)}, bf16[256,64]{0,1:T(8,128)(2,1)}, u32[]{:S(2)}) copy-start(bf16[256,64]{0,1:T(8,128)(2,1)} %param.15) | copy-start | bytes 98308
  5.7 0.8 %copy-start.5 = (bf16[256,64]{0,1:T(8,128)(2,1)S(1)}, bf16[256,64]{0,1:T(8,128)(2,1)}, u32[]{:S(2)}) copy-start(bf16[256,64]{0,1:T(8,128)(2,1)} %param.16) | copy-start | bytes 98308
  6.4 0.8 %copy-start.6 = (bf16[256,64]{0,1:T(8,128)(2,1)S(1)}, bf16[256,64]{0,1:T(8,128)(2,1)}, u32[]{:S(2)}) copy-start(bf16[256,64]{0,1:T(8,128)(2,1)} %param.17) | copy-start | bytes 98308
  7.2 0.7 %copy-start.8 = (bf16[256,8]{0,1:T(8,128)(2,1)S(1)}, bf16[256,8]{0,1:T(8,128)(2,1)}, u32[]{:S(2)}) copy-start(bf16[256,8]{0,1:T(8,128)(2,1)} %param.20) | copy-start | bytes 12292

commit v3 on v2

v3 whole, which is shorter than its diff:
```python
import functools

import jax
import jax.numpy as jnp
from jax import lax
from jax.experimental import pallas as pl
from jax.experimental.pallas import tpu as pltpu
from jax.sharding import PartitionSpec as P

MESH = pl.DeviceIdType.MESH
HEAD_DIMENSION = 32
XC = 8
EPS = 1e-05
BF = jnp.bfloat16
F32 = jnp.float32


def dot(a, b, ca, cb):
    return lax.dot_general(a, b, (((ca,), (cb,)), ((), ())), preferred_element_type=F32)


def standardize(v, gain):
    mean = jnp.mean(v, axis=-1, keepdims=True)
    centred = v - mean
    variance = jnp.mean(centred * centred, axis=-1, keepdims=True)
    return (centred * lax.rsqrt(variance + EPS) * gain).astype(BF)


def rem(a, n):
    return lax.rem(a, jnp.int32(n))


def div(a, n):
    return lax.div(a, jnp.int32(n))


def swap(src, tmp, store, a, b):
    for i in range(src.shape[-1] // 128):
        lanes = slice(i * 128, (i + 1) * 128)
        tmp[i] = src[..., lanes].astype(F32).reshape(a * b, 128)
        for k in range(b):
            store(k, lanes, tmp[i, pl.ds(k, a, stride=b), :].astype(BF))


def turn(mats):
    n = len(mats)
    width = mats[0].shape[1]
    lane = lax.broadcasted_iota(jnp.int32, (1, width), 1)
    mats = list(mats)
    dist = n // 2
    while dist >= 1:
        lanes = dist * (width // n)
        low = (lane // lanes) % 2 == 0
        out = list(mats)
        for r in range(n):
            if (r // dist) % 2 == 0:
                a, b = mats[r], mats[r + dist]
                out[r] = jnp.where(low, a, pltpu.roll(b, lanes, 1))
                out[r + dist] = jnp.where(low, pltpu.roll(a, width - lanes, 1), b)
        mats = out
        dist //= 2
    return mats


def kernel(
    dims,
    x_hbm, wq_hbm, wk_hbm, wv_hbm, wg_hbm, wo_hbm, gain1_hbm, gain2_hbm, f1_hbm, f2_hbm, pw_hbm, bias_hbm,
    o0_ref, o1_ref,
    wall, wo_ref, gain1_ref, gain2_ref, f1_ref, f2_ref, pw_ref, bias_ref, place,
    r1, r1c, tmp, s2, s2c, r2, mixed, acol, lcol, rcol, l1, tmpl, left, right, res, rx, ra1, tmpa, sa2, ra2,
    sem_s1, sem_r1, sem_s1c, sem_r1c, sem_sw, sem_rw, sem_sv, sem_rv, sem_s2, sem_s2c, sem_r2, sem_sl1, sem_rl1,
    sem_sl3, sem_rl3, sem_sr, sem_rr, sem_sa1, sem_ra1, sem_sa2, sem_ra2, sem_sa3, sem_ra3, sem_sx, sem_rx,
    sem_loc, sem_in,
):
    Z, H, CM = dims
    X = XC // 2
    H2 = H // 2
    G = 2 * Z
    S = G * XC
    N = S * H
    HW = wq_hbm.shape[0]
    NH = HW // HEAD_DIMENSION
    FC = f1_hbm.shape[0]
    CC = f2_hbm.shape[0]
    CZ = pw_hbm.shape[1]
    WR = wall.shape[1] // 2
    d = lax.axis_index("dap")
    h = lax.axis_index("head")
    z = div(d, 2 * XC)
    yh = rem(div(d, XC), 2)
    xc = rem(d, XC)
    xx = div(xc, 2)
    core = rem(xc, 2)
    oy = 1 - yh
    block = (z * 2 + yh) * XC
    cross = (z * 2 + oy) * XC
    sib = block + 2 * xx + (1 - core)
    edge = (h == 0) | (h == H - 1)
    lo = jnp.where(h == 0, H2, 0)
    h_src = jnp.where(h < H2, H - 1, 0)

    def rcopy(src, dst, ssem, rsem, dd, hh):
        return pltpu.make_async_remote_copy(
            src_ref=src, dst_ref=dst, send_sem=ssem, recv_sem=rsem, device_id=(dd, hh), device_id_type=MESH
        )

    def each(n, f, first=1):
        def step(o, c):
            f(o)
            return c

        if n > first:
            lax.fori_loop(first, n, step, 0)

    def zz(o):
        return rem(z + o, Z)

    def dz(o):
        return (zz(o) * 2 + yh) * XC + xc

    def dm(o):
        return (zz(o) * 2 + oy) * XC + xc

    def tx(o):
        return rem(xc + o, XC)

    def th(o):
        return rem(h + o, H)

    barrier = pltpu.get_barrier_semaphore()

    def signal(dd, hh):
        pl.semaphore_signal(barrier, inc=1, device_id=(dd, hh), device_id_type=MESH)

    for o in range(1, XC):
        signal(block + tx(o), h)
    for o in range(1, Z):
        signal(dz(o), h)
    for o in range(Z):
        signal(dm(o), H - 1 - h)
    for o in range(XC):
        signal(cross + o, h_src)
    for o in range(H):
        signal(cross + xc, o)
    for k in range(1, H):
        hh = th(k)
        for o in range(XC):
            signal(block + o, hh)

    ins = [
        pltpu.make_async_copy(w, wall.at[h, pl.ds(i * HW, HW)], sem_in.at[i])
        for i, w in enumerate((wq_hbm, wk_hbm, wv_hbm, wg_hbm))
    ]
    for w, ref in (
        (f1_hbm, f1_ref), (f2_hbm, f2_ref), (gain1_hbm, gain1_ref), (gain2_hbm, gain2_ref), (wo_hbm, wo_ref),
        (bias_hbm, bias_ref), (pw_hbm, pw_ref),
    ):
        ins.append(pltpu.make_async_copy(w, ref, sem_in.at[len(ins)]))
    for copy in ins:
        copy.start()
    loc1 = pltpu.make_async_copy(x_hbm.at[z, yh, h], r1.at[z], sem_loc.at[0])
    loc1c = pltpu.make_async_copy(x_hbm.at[z, oy, pl.ds(lo, H2)], r1c.at[z], sem_loc.at[1])
    loc1.start()
    loc1c.start()

    pl.semaphore_wait(barrier, (Z - 1) + Z + (XC * H - 1) + H + jnp.where(edge, XC * H2, 0))

    def a1(o):
        t = zz(o)
        return rcopy(x_hbm.at[t, yh, h], r1.at[z], sem_s1.at[t], sem_r1.at[z], dz(o), h)

    def a1c(o):
        t = zz(o)
        return rcopy(x_hbm.at[t, oy, pl.ds(lo, H2)], r1c.at[z], sem_s1c.at[t], sem_r1c.at[z], dz(o), h)

    @pl.when(edge)
    def _():
        each(Z, lambda o: a1c(o).start())

    each(Z, lambda o: a1(o).start())

    for copy in ins[:5]:
        copy.wait()
    wall[h, 4 * HW :, :] = jnp.concatenate(
        [f1_ref[...].astype(F32), jnp.zeros((2 * WR - 4 * HW - FC, CM), F32)], axis=0
    ).astype(BF)
    half = pl.ds(pl.multiple_of(core * WR, 16), WR)
    other = pl.ds(pl.multiple_of((1 - core) * WR, 16), WR)

    def aw(o):
        hh = th(o)
        return rcopy(wall.at[h, half], wall.at[h, half], sem_sw.at[hh], sem_rw.at[h], d, hh)

    each(H, lambda o: aw(o).start())

    for copy in ins[5:]:
        copy.wait()

    def wait_r1(o):
        t = zz(o)
        rcopy(x_hbm.at[t, yh, h], r1.at[t], sem_s1.at[t], sem_r1.at[t], dz(o), h).wait_recv()

    def wait_r1c(o):
        t = zz(o)
        rcopy(x_hbm.at[t, oy, pl.ds(lo, H2)], r1c.at[t], sem_s1c.at[t], sem_r1c.at[t], dz(o), h).wait_recv()

    loc1.wait()
    loc1c.wait()

    def a2c(i, t):
        return rcopy(
            s2c.at[i, t], r2.at[yh, xc], sem_s2c.at[i * XC + t], sem_r2.at[yh * XC + xc], cross + t, lo + i
        )

    @pl.when(edge)
    def _():
        each(Z, wait_r1c)
        for i in range(H2):

            def store(k, lanes, v):
                s2c[i, k, :, lanes] = v

            swap(r1c.at[:, i], tmp, store, Z, XC)
            each(XC, lambda t: a2c(i, t).start(), 0)

    each(Z, wait_r1)

    def store_s2(k, lanes, v):
        s2[k, :, lanes] = v

    swap(r1, tmp, store_s2, Z, XC)

    def a2(o):
        t = tx(o)
        return rcopy(s2.at[t], r2.at[yh, xc], sem_s2.at[t], sem_r2.at[yh * XC + xc], block + t, h)

    each(XC, lambda o: a2(o).start())
    r2[yh, xc] = s2[xc]

    row = lax.broadcasted_iota(jnp.int32, (N, 1), 0)
    src = row // (2 * G)
    mirror = (row // Z) % 2
    src_h = jnp.where(mirror == 1, H - 1 - src % H, src % H)
    src_y = jnp.where(mirror == 1, oy, yh)
    at = ((row % Z) * 2 + src_y) * (H * XC) + src_h * XC + (src // H) * 2 + (row // G) % 2
    place[...] = jnp.where(lax.broadcasted_iota(jnp.int32, (N, N), 1) == at, 1.0, 0.0).astype(BF)

    def wait_r2(o):
        t = tx(o)
        rcopy(s2.at[t], r2.at[yh, t], sem_s2.at[t], sem_r2.at[yh * XC + t], block + t, h).wait_recv()

    def wait_r2c(t):
        rcopy(s2.at[t], r2.at[oy, t], sem_s2.at[t], sem_r2.at[oy * XC + t], cross + t, h_src).wait_recv()

    each(XC, wait_r2)
    each(XC, wait_r2c, 0)

    def av(o):
        hh = th(o)
        return rcopy(wall.at[hh, half], wall.at[hh, half], sem_sv.at[hh], sem_rv.at[hh], sib, h)

    def pass_w(o):
        hh = th(o)
        rcopy(wall.at[hh, half], wall.at[hh, half], sem_sw.at[hh], sem_rw.at[hh], d, hh).wait_recv()
        av(o).start()

    each(H, pass_w)
    activity = r2[...].astype(F32).reshape(S, CM)
    normed = standardize(activity, gain1_ref[...])

    for o in range(H):
        hh = th(o)
        if o > 0:
            rcopy(wall.at[hh, other], wall.at[hh, other], sem_sv.at[hh], sem_rv.at[hh], sib, h).wait_recv()
        proj = dot(wall[hh, : 4 * HW, :], normed, 1, 1)
        query = proj[:HW].astype(BF)
        keys = proj[HW : 2 * HW].astype(BF)
        values = proj[2 * HW : 3 * HW].astype(BF)
        gate = jax.nn.sigmoid(proj[3 * HW :]).astype(BF).astype(F32)
        parts = []
        for e in range(NH):
            rows = slice(e * HEAD_DIMENSION, (e + 1) * HEAD_DIMENSION)
            scores = dot(keys[rows], query[rows], 0, 0) * HEAD_DIMENSION ** (-0.5)
            weights = jnp.exp(scores - jnp.max(scores, axis=0, keepdims=True))
            probs = (weights / jnp.sum(weights, axis=0, keepdims=True)).astype(BF)
            parts.append((dot(values[rows], probs, 1, 0) * gate[rows]).astype(BF))
        mixed[pl.ds(pl.multiple_of(hh * HW, HW), HW), :] = jnp.concatenate(parts, axis=0)
    after = (activity + dot(mixed[...], wo_ref[...], 0, 0)).astype(BF).astype(F32)
    acol[...] = after.reshape(2, XC, Z, CM).astype(BF)
    normed2 = standardize(after, gain2_ref[...])
    f1 = jnp.concatenate([wall[k, 4 * HW :, :].astype(F32)[:FC] for k in range(H)], axis=0).astype(BF)
    lcol[...] = dot(f1, normed2, 1, 1).astype(BF)
    rcol[...] = dot(f2_ref[...], normed2, 1, 1).astype(BF)

    def al1(o):
        return rcopy(lcol, l1.at[z], sem_sl1.at[o], sem_rl1.at[z], dz(o), h)

    def al1m(o):
        return rcopy(lcol, l1.at[Z + z], sem_sl1.at[Z + o], sem_rl1.at[Z + z], dm(o), H - 1 - h)

    each(Z, lambda o: al1m(o).start(), 0)
    each(Z, lambda o: al1(o).start())
    l1[z] = lcol[...]

    core_d = div(xc, H)
    slot = h * H + rem(xc, H)

    def ar(o):
        x2 = rem(xx + div(o, H), X)
        return rcopy(rcol, right.at[slot], sem_sr.at[o], sem_rr.at[slot], block + 2 * x2 + core_d, th(rem(o, H)))

    @pl.when(core == core_d)
    def _():
        right[slot] = rcol[...]

    @pl.when(core != core_d)
    def _():
        ar(jnp.int32(0)).start()

    each(X * H, lambda o: ar(o).start())

    def aa1(o):
        t = tx(o)
        return rcopy(acol.at[:, t], ra1.at[xc], sem_sa1.at[t], sem_ra1.at[xc], block + t, h)

    each(XC, lambda o: aa1(o).start())
    ra1[xc] = acol[:, xc]

    def wait_a1(o):
        t = tx(o)
        rcopy(acol.at[:, t], ra1.at[t], sem_sa1.at[t], sem_ra1.at[t], block + t, h).wait_recv()

    each(XC, wait_a1)

    def store_a2(k, lanes, v):
        sa2[k // Z, k % Z, :, lanes] = v

    swap(ra1, tmpa, store_a2, XC, G)

    def aa2(o):
        t = zz(o)
        return rcopy(sa2.at[:, t], ra2.at[:, z], sem_sa2.at[t], sem_ra2.at[z], dz(o), h)

    each(Z, lambda o: aa2(o).start())
    ra2[:, z] = sa2[:, z]

    def wait_l1(k):
        rcopy(lcol, l1.at[k], sem_sl1.at[0], sem_rl1.at[k], d, h).wait_recv()

    each(Z, lambda o: wait_l1(zz(o)))
    each(Z, lambda o: wait_l1(Z + o), 0)
    tmpl[...] = l1[...].astype(F32).reshape(G * CC, S)
    for c in range(CC):
        left[0, c] = tmpl[pl.ds(c, G, stride=CC), :].astype(BF)
    al3 = rcopy(left.at[0], left.at[1], sem_sl3, sem_rl3, sib, h)
    al3.start()

    for k in range(X * H):
        from_h, from_xc = k // H, core * H + k % H

        @pl.when(jnp.logical_not((from_h == h) & (from_xc == xc)))
        def _():
            rcopy(rcol, right.at[k], sem_sr.at[0], sem_rr.at[k], block + from_xc, from_h).wait_recv()

    own = xx * H + h

    def ax(side, x2, hh):
        k = (side * X + x2) * H + hh
        at_core = core if side == 0 else 1 - core
        return rcopy(
            res.at[side, x2 * H + hh], rx.at[own, at_core], sem_sx.at[k], sem_rx.at[own * 2 + at_core],
            block + 2 * x2 + core, hh,
        )

    def pair_half(side):
        lefts = left[side].reshape(CC * G, S)
        flats = []
        for x2 in range(X):
            outer = dot(lefts, right[x2 * H : (x2 + 1) * H].reshape(H * CC, S), 1, 1) * (1.0 / S)
            flat = [[] for _ in range(H)]
            for c in range(0, CC, H):
                for k, part in enumerate(turn([outer[(c + r) * G : (c + r + 1) * G] for r in range(H)])):
                    flat[k].append(part.astype(BF))
            flats += [jnp.concatenate(f, axis=1) for f in flat]
        total = jnp.dot(jnp.concatenate(flats, axis=0), pw_ref[...], preferred_element_type=F32) + bias_ref[...]
        for x2 in range(X):
            base = x2 * H * G
            for hh, part in enumerate(turn([total[base + k * G : base + (k + 1) * G] for k in range(H)])):
                res[side, x2 * H + hh] = part.astype(BF)
                here = (x2 == xx) & (hh == h)

                @pl.when(here)
                def _():
                    rx[own, core if side == 0 else 1 - core] = res[side, x2 * H + hh]

                @pl.when(jnp.logical_not(here))
                def _():
                    ax(side, x2, hh).start()

    pair_half(0)

    def wait_a2(o):
        t = zz(o)
        rcopy(sa2.at[:, t], ra2.at[:, t], sem_sa2.at[t], sem_ra2.at[t], dz(o), h).wait_recv()

    each(Z, wait_a2)

    def aa3(o):
        return rcopy(
            ra2.at[yh], o0_ref.at[:, yh, h], sem_sa3.at[o], sem_ra3.at[yh * H + h], block + xc, th(o)
        )

    def aa3c(o):
        return rcopy(
            ra2.at[oy], o0_ref.at[:, yh, h], sem_sa3.at[H + o], sem_ra3.at[yh * H + h], cross + xc, o
        )

    each(H, lambda o: aa3c(o).start(), 0)
    each(H, lambda o: aa3(o).start())
    o0_ref[:, yh, h] = ra2[yh]

    rcopy(left.at[0], left.at[1], sem_sl3, sem_rl3, sib, h).wait_recv()
    pair_half(1)

    for x2 in range(X):
        for hh in range(H):
            k = x2 * H + hh

            @pl.when(k != own)
            def _():
                for c in range(2):
                    rcopy(
                        res.at[0, k], rx.at[k, c], sem_sx.at[k], sem_rx.at[k * 2 + c], block + 2 * x2 + core, hh
                    ).wait_recv()

    o1_ref[...] = dot(rx[...].reshape(N, CZ), place[...], 0, 0).astype(BF)

    def wait_a3(o):
        hh = th(o)
        rcopy(ra2.at[yh], o0_ref.at[:, yh, hh], sem_sa3.at[o], sem_ra3.at[yh * H + hh], d, hh).wait_recv()

    def wait_a3c(o):
        rcopy(ra2.at[oy], o0_ref.at[:, oy, o], sem_sa3.at[H + o], sem_ra3.at[oy * H + o], cross + xc, o).wait_recv()

    each(H, wait_a3)
    each(H, wait_a3c, 0)
    each(Z, lambda o: a1(o).wait_send())

    @pl.when(edge)
    def _():
        each(Z, lambda o: a1c(o).wait_send())
        for i in range(H2):
            each(XC, lambda t: a2c(i, t).wait_send(), 0)

    each(H, lambda o: aw(o).wait_send())
    each(H, lambda o: av(o).wait_send())
    each(XC, lambda o: a2(o).wait_send())
    each(Z, lambda o: al1m(o).wait_send(), 0)
    each(Z, lambda o: al1(o).wait_send())

    @pl.when(core != core_d)
    def _():
        ar(jnp.int32(0)).wait_send()

    each(X * H, lambda o: ar(o).wait_send())
    each(XC, lambda o: aa1(o).wait_send())
    each(Z, lambda o: aa2(o).wait_send())
    al3.wait_send()
    each(H, lambda o: aa3c(o).wait_send(), 0)
    each(H, lambda o: aa3(o).wait_send())
    for side in range(2):
        for x2 in range(X):
            for hh in range(H):

                @pl.when(x2 * H + hh != own)
                def _():
                    ax(side, x2, hh).wait_send()


def shards(mesh, x, gain1, wq, wk, wv, wg, wo, gain2, f1, f2, pw, bias):
    D, H = mesh.shape["dap"], mesh.shape["head"]
    G, X = D // XC, XC // 2
    Z = G // 2
    S = D
    CM = x.shape[2]
    HW, FC, CC, CZ = wq.shape[1], f1.shape[1], f2.shape[1], pw.shape[1]
    vm = pl.BlockSpec(memory_space=pltpu.VMEM)
    hbm = pl.BlockSpec(memory_space=pltpu.HBM)
    dma = pltpu.SemaphoreType.DMA
    scratch = [
        pltpu.VMEM((H, 4 * HW + 32, CM), BF),
        pltpu.VMEM((CM, CM), BF),
        pltpu.VMEM((1, CM), F32),
        pltpu.VMEM((1, CM), F32),
        pltpu.VMEM((FC, CM), BF),
        pltpu.VMEM((CC, CM), BF),
        pltpu.VMEM((CC * CC, CZ), BF),
        pltpu.VMEM((1, CZ), F32),
        pltpu.VMEM((S * H, S * H), BF),
        pltpu.VMEM((Z, XC, CM), BF),
        pltpu.VMEM((Z, H // 2, XC, CM), BF),
        pltpu.VMEM((CM // 128, Z * XC, 128), F32),
        pltpu.VMEM((XC, Z, CM), BF),
        pltpu.VMEM((H // 2, XC, Z, CM), BF),
        pltpu.VMEM((2, XC, Z, CM), BF),
        pltpu.VMEM((CM, S), BF),
        pltpu.VMEM((2, XC, Z, CM), BF),
        pltpu.VMEM((CC, S), BF),
        pltpu.VMEM((CC, S), BF),
        pltpu.VMEM((G, CC, S), BF),
        pltpu.VMEM((G * CC, S), F32),
        pltpu.VMEM((2, CC, G, S), BF),
        pltpu.VMEM((X * H, CC, S), BF),
        pltpu.VMEM((2, X * H, G, CZ), BF),
        pltpu.VMEM((X * H, 2, G, CZ), BF),
        pltpu.VMEM((XC, 2, Z, CM), BF),
        pltpu.VMEM((CM // 128, S, 128), F32),
        pltpu.VMEM((2, Z, XC, CM), BF),
        pltpu.VMEM((2, Z, XC, CM), BF),
    ]
    sems = [
        Z, Z, Z, Z, H, H, H, H, XC, H // 2 * XC, 2 * XC, G, G,
        None, None, X * H, X * H, XC, XC, Z, Z, 2 * H, 2 * H, 2 * X * H, 2 * X * H,
        2, 11,
    ]
    scratch += [dma if n is None else dma((n,)) for n in sems]
    o0, o1 = pl.pallas_call(
        functools.partial(kernel, (Z, H, CM)),
        out_shape=(
            pltpu.VMEM((Z, 2, H, XC, CM), BF),
            pltpu.VMEM((CZ, H * S), BF),
        ),
        in_specs=[hbm] * 12,
        out_specs=(vm, vm),
        scratch_shapes=scratch,
        compiler_params=pltpu.CompilerParams(
            collective_id=0, has_side_effects=True, vmem_limit_bytes=60 * 1024 * 1024
        ),
    )(
        x.reshape(Z, 2, H, XC, CM), wq.T, wk.T, wv.T, wg.T, wo, gain1.reshape(1, CM), gain2.reshape(1, CM), f1.T, f2.T,
        pw, bias.reshape(1, CZ),
    )
    return o0.reshape(1, H * S, CM), o1.reshape(H, CZ // H, H * S).transpose(2, 0, 1)


def solution(mesh):
    placed = (
        P("dap", None, None),
        P(),
        P(None, "head"),
        P(None, "head"),
        P(None, "head"),
        P(None, "head"),
        P(),
        P(),
        P(None, "head"),
        P(),
        P(),
        P(),
    )
    return jax.shard_map(
        functools.partial(shards, mesh),
        mesh=mesh,
        in_specs=placed,
        out_specs=(P("dap", None, None), P(None, "dap", "head")),
        check_vma=False,
    )
```

time: 68.2 us -> 55.3 us (0.81)
  local copies, waits for them, and re-layouts: 8.57 us -> 1.36 us
  Pallas kernels: 58.4 us -> 53.2 us
    unnamed x26 -> x2, local copies, waits for them, and re-layouts: 8.57 us -> 1.36 us
    pallas_call x1, Pallas kernels: 58.4 us -> 53.2 us  [shards(): pl.pallas_call(functools.partial(kernel, (Z, H, CM)), out_shape=(pltpu.VM...]
where the time goes in v3:
time: 55.3 us; the launch traced here: 55.2 us
  Pallas kernels  53.2 us (96%)
  local copies, waits for them, and re-layouts  1.36 us (2%)
  between operations  0.64 us (1%)
    pallas_call x1, Pallas kernels, shards(): pl.pallas_call(functools.partial(kernel, (Z, H, CM)), out_shape=(pltpu.VM...  53.2 us
    unnamed x2, local copies, waits for them, and re-layouts  1.36 us

profile of v3, /device:TPU:1, one launch (start us, length us, event | category | flops | bytes accessed | tf_op | source)
XLA Modules:
  0.0 55.2 jit_solution(8210406592439657095)
XLA Ops:
  0.6 53.2 %shard_map.131 = (bf16[8,2,4,8,256]{4,3,2,1,0:T(8,128)(2,1)S(1)}, bf16[128,512]{1,0:T(8,128)(2,1)S(1)}) custom-call(bf16[8,2,4,8,256]{4,3,2,1,0:T(8,128)(2,1)} %bitcast.16, bf16[64,256]{1,0:T(8,128)(2,1)} %bitcast.17, bf16[64,256]{1,0:T(8,128)(2,1)} %bitcast.18, bf16[64,256]{1,0:T(8,128)(2,1)} %bitcast.19, bf16[64,256]{1,0:T(8,128)(2,1)} %bitcast.20, ...), custom_call_target="tpu_custom_call" | custom-call | tf_op jit(solution)/shard_map/pallas_call | solution.py:527
  53.8 0.7 %copy.16 = bf16[1,512,256]{2,1,0:T(8,128)(2,1)} copy(bf16[1,512,256]{2,1,0:T(8,128)(2,1)S(1)} %bitcast.14) | data formatting | bytes 524288
  54.5 0.7 %copy.17 = bf16[512,4,32]{0,2,1:T(8,128)(2,1)} copy(bf16[512,4,32]{0,2,1:T(8,128)(2,1)S(1)} %bitcast.15) | data formatting | bytes 262144

commit v4 on v3

--- a/solution.py
+++ b/solution.py
@@ -67,10 +67,10 @@
     x_hbm, wq_hbm, wk_hbm, wv_hbm, wg_hbm, wo_hbm, gain1_hbm, gain2_hbm, f1_hbm, f2_hbm, pw_hbm, bias_hbm,
     o0_ref, o1_ref,
     wall, wo_ref, gain1_ref, gain2_ref, f1_ref, f2_ref, pw_ref, bias_ref, place,
-    r1, r1c, tmp, s2, s2c, r2, mixed, acol, lcol, rcol, l1, tmpl, left, right, res, rx, ra1, tmpa, sa2, ra2,
+    xs, xsc, r1, r1c, tmp, s2, s2c, r2, mixed, acol, lcol, rcol, l1, tmpl, left, right, res, rx, ra1, tmpa, sa2, ra2,
     sem_s1, sem_r1, sem_s1c, sem_r1c, sem_sw, sem_rw, sem_sv, sem_rv, sem_s2, sem_s2c, sem_r2, sem_sl1, sem_rl1,
     sem_sl3, sem_rl3, sem_sr, sem_rr, sem_sa1, sem_ra1, sem_sa2, sem_ra2, sem_sa3, sem_ra3, sem_sx, sem_rx,
-    sem_loc, sem_in,
+    sem_loc, sem_in, ready,
 ):
     Z, H, CM = dims
     X = XC // 2
@@ -132,12 +132,10 @@
     def signal(dd, hh):
         pl.semaphore_signal(barrier, inc=1, device_id=(dd, hh), device_id_type=MESH)
 
+    for o in sorted(range(1, Z), key=lambda o: -min(o, Z - o)):
+        signal(dz(o), h)
     for o in range(1, XC):
         signal(block + tx(o), h)
-    for o in range(1, Z):
-        signal(dz(o), h)
-    for o in range(Z):
-        signal(dm(o), H - 1 - h)
     for o in range(XC):
         signal(cross + o, h_src)
     for o in range(H):
@@ -147,6 +145,10 @@
         for o in range(XC):
             signal(block + o, hh)
 
+    loc1 = pltpu.make_async_copy(x_hbm.at[:, yh, h], xs, sem_loc.at[0])
+    loc1c = pltpu.make_async_copy(x_hbm.at[:, oy, pl.ds(lo, H2)], xsc, sem_loc.at[1])
+    loc1.start()
+    loc1c.start()
     ins = [
         pltpu.make_async_copy(w, wall.at[h, pl.ds(i * HW, HW)], sem_in.at[i])
         for i, w in enumerate((wq_hbm, wk_hbm, wv_hbm, wg_hbm))
@@ -158,26 +160,27 @@
         ins.append(pltpu.make_async_copy(w, ref, sem_in.at[len(ins)]))
     for copy in ins:
         copy.start()
-    loc1 = pltpu.make_async_copy(x_hbm.at[z, yh, h], r1.at[z], sem_loc.at[0])
-    loc1c = pltpu.make_async_copy(x_hbm.at[z, oy, pl.ds(lo, H2)], r1c.at[z], sem_loc.at[1])
-    loc1.start()
-    loc1c.start()
-
-    pl.semaphore_wait(barrier, (Z - 1) + Z + (XC * H - 1) + H + jnp.where(edge, XC * H2, 0))
+
+    pl.semaphore_wait(barrier, (Z - 1) + (XC * H - 1) + H + jnp.where(edge, XC * H2, 0))
+    loc1.wait()
+    loc1c.wait()
 
     def a1(o):
         t = zz(o)
-        return rcopy(x_hbm.at[t, yh, h], r1.at[z], sem_s1.at[t], sem_r1.at[z], dz(o), h)
+        return rcopy(xs.at[t], r1.at[z], sem_s1.at[t], sem_r1.at[z], dz(o), h)
 
     def a1c(o):
         t = zz(o)
-        return rcopy(x_hbm.at[t, oy, pl.ds(lo, H2)], r1c.at[z], sem_s1c.at[t], sem_r1c.at[z], dz(o), h)
+        return rcopy(xsc.at[t], r1c.at[z], sem_s1c.at[t], sem_r1c.at[z], dz(o), h)
 
     @pl.when(edge)
     def _():
         each(Z, lambda o: a1c(o).start())
 
     each(Z, lambda o: a1(o).start())
+    pl.semaphore_signal(ready, inc=1, device_id=(cross + xc, H - 1 - h), device_id_type=MESH)
+    r1[z] = xs[z]
+    r1c[z] = xsc[z]
 
     for copy in ins[:5]:
         copy.wait()
@@ -198,14 +201,11 @@
 
     def wait_r1(o):
         t = zz(o)
-        rcopy(x_hbm.at[t, yh, h], r1.at[t], sem_s1.at[t], sem_r1.at[t], dz(o), h).wait_recv()
+        rcopy(xs.at[t], r1.at[t], sem_s1.at[t], sem_r1.at[t], dz(o), h).wait_recv()
 
     def wait_r1c(o):
         t = zz(o)
-        rcopy(x_hbm.at[t, oy, pl.ds(lo, H2)], r1c.at[t], sem_s1c.at[t], sem_r1c.at[t], dz(o), h).wait_recv()
-
-    loc1.wait()
-    loc1c.wait()
+        rcopy(xsc.at[t], r1c.at[t], sem_s1c.at[t], sem_r1c.at[t], dz(o), h).wait_recv()
 
     def a2c(i, t):
         return rcopy(
@@ -287,6 +287,13 @@
         mixed[pl.ds(pl.multiple_of(hh * HW, HW), HW), :] = jnp.concatenate(parts, axis=0)
     after = (activity + dot(mixed[...], wo_ref[...], 0, 0)).astype(BF).astype(F32)
     acol[...] = after.reshape(2, XC, Z, CM).astype(BF)
+    def aa1(o):
+        t = tx(o)
+        return rcopy(acol.at[:, t], ra1.at[xc], sem_sa1.at[t], sem_ra1.at[xc], block + t, h)
+
+    each(XC, lambda o: aa1(o).start())
+    ra1[xc] = acol[:, xc]
+
     normed2 = standardize(after, gain2_ref[...])
     f1 = jnp.concatenate([wall[k, 4 * HW :, :].astype(F32)[:FC] for k in range(H)], axis=0).astype(BF)
     lcol[...] = dot(f1, normed2, 1, 1).astype(BF)
@@ -298,6 +305,7 @@
     def al1m(o):
         return rcopy(lcol, l1.at[Z + z], sem_sl1.at[Z + o], sem_rl1.at[Z + z], dm(o), H - 1 - h)
 
+    pl.semaphore_wait(ready, 1)
     each(Z, lambda o: al1m(o).start(), 0)
     each(Z, lambda o: al1(o).start())
     l1[z] = lcol[...]
@@ -319,13 +327,6 @@
 
     each(X * H, lambda o: ar(o).start())
 
-    def aa1(o):
-        t = tx(o)
-        return rcopy(acol.at[:, t], ra1.at[xc], sem_sa1.at[t], sem_ra1.at[xc], block + t, h)
-
-    each(XC, lambda o: aa1(o).start())
-    ra1[xc] = acol[:, xc]
-
     def wait_a1(o):
         t = tx(o)
         rcopy(acol.at[:, t], ra1.at[t], sem_sa1.at[t], sem_ra1.at[t], block + t, h).wait_recv()
@@ -343,6 +344,28 @@
 
     each(Z, lambda o: aa2(o).start())
     ra2[:, z] = sa2[:, z]
+
+    def aa3(t, o):
+        return rcopy(
+            ra2.at[yh, t], o0_ref.at[t, yh, h], sem_sa3.at[o], sem_ra3.at[yh * H + h], block + xc, th(o)
+        )
+
+    def aa3c(t, o):
+        return rcopy(
+            ra2.at[oy, t], o0_ref.at[t, yh, h], sem_sa3.at[H + o], sem_ra3.at[yh * H + h], cross + xc, o
+        )
+
+    def ring(t):
+        each(H, lambda o: aa3c(t, o).start(), 0)
+        each(H, lambda o: aa3(t, o).start())
+
+    def wait_a2(o):
+        t = zz(o)
+        rcopy(sa2.at[:, t], ra2.at[:, t], sem_sa2.at[t], sem_ra2.at[t], dz(o), h).wait_recv()
+        ring(t)
+
+    near = sorted(range(1, Z), key=lambda o: min(o, Z - o))
+    ring(z)
 
     def wait_l1(k):
         rcopy(lcol, l1.at[k], sem_sl1.at[0], sem_rl1.at[k], d, h).wait_recv()
@@ -397,26 +420,11 @@
                 def _():
                     ax(side, x2, hh).start()
 
+    for o in near[:4]:
+        wait_a2(o)
     pair_half(0)
-
-    def wait_a2(o):
-        t = zz(o)
-        rcopy(sa2.at[:, t], ra2.at[:, t], sem_sa2.at[t], sem_ra2.at[t], dz(o), h).wait_recv()
-
-    each(Z, wait_a2)
-
-    def aa3(o):
-        return rcopy(
-            ra2.at[yh], o0_ref.at[:, yh, h], sem_sa3.at[o], sem_ra3.at[yh * H + h], block + xc, th(o)
-        )
-
-    def aa3c(o):
-        return rcopy(
-            ra2.at[oy], o0_ref.at[:, yh, h], sem_sa3.at[H + o], sem_ra3.at[yh * H + h], cross + xc, o
-        )
-
-    each(H, lambda o: aa3c(o).start(), 0)
-    each(H, lambda o: aa3(o).start())
+    for o in near[4:]:
+        wait_a2(o)
     o0_ref[:, yh, h] = ra2[yh]
 
     rcopy(left.at[0], left.at[1], sem_sl3, sem_rl3, sib, h).wait_recv()
@@ -437,10 +445,10 @@
 
     def wait_a3(o):
         hh = th(o)
-        rcopy(ra2.at[yh], o0_ref.at[:, yh, hh], sem_sa3.at[o], sem_ra3.at[yh * H + hh], d, hh).wait_recv()
+        rcopy(ra2.at[yh], o0_ref.at[:, yh, hh], sem_sa3.at[o], sem_ra3.at[yh * H + hh], d, hh).wait()
 
     def wait_a3c(o):
-        rcopy(ra2.at[oy], o0_ref.at[:, oy, o], sem_sa3.at[H + o], sem_ra3.at[oy * H + o], cross + xc, o).wait_recv()
+        rcopy(ra2.at[oy], o0_ref.at[:, oy, o], sem_sa3.at[H + o], sem_ra3.at[oy * H + o], cross + xc, o).wait()
 
     each(H, wait_a3)
     each(H, wait_a3c, 0)
@@ -466,8 +474,6 @@
     each(XC, lambda o: aa1(o).wait_send())
     each(Z, lambda o: aa2(o).wait_send())
     al3.wait_send()
-    each(H, lambda o: aa3c(o).wait_send(), 0)
-    each(H, lambda o: aa3(o).wait_send())
     for side in range(2):
         for x2 in range(X):
             for hh in range(H):
@@ -497,6 +503,8 @@
         pltpu.VMEM((CC * CC, CZ), BF),
         pltpu.VMEM((1, CZ), F32),
         pltpu.VMEM((S * H, S * H), BF),
+        pltpu.VMEM((Z, XC, CM), BF),
+        pltpu.VMEM((Z, H // 2, XC, CM), BF),
         pltpu.VMEM((Z, XC, CM), BF),
         pltpu.VMEM((Z, H // 2, XC, CM), BF),
         pltpu.VMEM((CM // 128, Z * XC, 128), F32),
@@ -524,6 +532,7 @@
         2, 11,
     ]
     scratch += [dma if n is None else dma((n,)) for n in sems]
+    scratch.append(pltpu.SemaphoreType.REGULAR)
     o0, o1 = pl.pallas_call(
         functools.partial(kernel, (Z, H, CM)),
         out_shape=(

time: 55.3 us -> 52.8 us (0.955)
  Pallas kernels: 53.2 us -> 50.6 us
    pallas_call x1, Pallas kernels: 53.2 us -> 50.6 us  [shards(): pl.pallas_call(functools.partial(kernel, (Z, H, CM)), out_shape=(pltpu.VM...]
where the time goes in v4:
time: 52.8 us; the launch traced here: 52.6 us
  Pallas kernels  50.6 us (96%)
  local copies, waits for them, and re-layouts  1.36 us (3%)
  between operations  0.64 us (1%)
    pallas_call x1, Pallas kernels, shards(): pl.pallas_call(functools.partial(kernel, (Z, H, CM)), out_shape=(pltpu.VM...  50.6 us
    unnamed x2, local copies, waits for them, and re-layouts  1.36 us

profile of v4, /device:TPU:1, one launch (start us, length us, event | category | flops | bytes accessed | tf_op | source)
XLA Modules:
  0.0 52.6 jit_solution(4185923167272977614)
XLA Ops:
  0.6 50.6 %shard_map.131 = (bf16[8,2,4,8,256]{4,3,2,1,0:T(8,128)(2,1)S(1)}, bf16[128,512]{1,0:T(8,128)(2,1)S(1)}) custom-call(bf16[8,2,4,8,256]{4,3,2,1,0:T(8,128)(2,1)} %bitcast.16, bf16[64,256]{1,0:T(8,128)(2,1)} %bitcast.17, bf16[64,256]{1,0:T(8,128)(2,1)} %bitcast.18, bf16[64,256]{1,0:T(8,128)(2,1)} %bitcast.19, bf16[64,256]{1,0:T(8,128)(2,1)} %bitcast.20, ...), custom_call_target="tpu_custom_call" | custom-call | tf_op jit(solution)/shard_map/pallas_call | solution.py:536
  51.3 0.7 %copy.16 = bf16[1,512,256]{2,1,0:T(8,128)(2,1)} copy(bf16[1,512,256]{2,1,0:T(8,128)(2,1)S(1)} %bitcast.14) | data formatting | bytes 524288
  52.0 0.7 %copy.17 = bf16[512,4,32]{0,2,1:T(8,128)(2,1)} copy(bf16[512,4,32]{0,2,1:T(8,128)(2,1)S(1)} %bitcast.15) | data formatting | bytes 262144

commit v5 on v4

--- a/solution.py
+++ b/solution.py
@@ -67,9 +67,9 @@
     x_hbm, wq_hbm, wk_hbm, wv_hbm, wg_hbm, wo_hbm, gain1_hbm, gain2_hbm, f1_hbm, f2_hbm, pw_hbm, bias_hbm,
     o0_ref, o1_ref,
     wall, wo_ref, gain1_ref, gain2_ref, f1_ref, f2_ref, pw_ref, bias_ref, place,
-    xs, xsc, r1, r1c, tmp, s2, s2c, r2, mixed, acol, lcol, rcol, l1, tmpl, left, right, res, rx, ra1, tmpa, sa2, ra2,
+    xs, xsc, r1, r1c, tmp, s2, s2c, r2, mixed, acol, lcol, rcol, l1, tmpl, left, rights, right, res, rx, ra1, tmpa, sa2, ra2,
     sem_s1, sem_r1, sem_s1c, sem_r1c, sem_sw, sem_rw, sem_sv, sem_rv, sem_s2, sem_s2c, sem_r2, sem_sl1, sem_rl1,
-    sem_sl3, sem_rl3, sem_sr, sem_rr, sem_sa1, sem_ra1, sem_sa2, sem_ra2, sem_sa3, sem_ra3, sem_sx, sem_rx,
+    sem_sl3, sem_rl3, sem_sr, sem_rr, sem_sq, sem_rq, sem_sa1, sem_ra1, sem_sa2, sem_ra2, sem_sa3, sem_ra3, sem_sx, sem_rx,
     sem_loc, sem_in, ready,
 ):
     Z, H, CM = dims
@@ -112,6 +112,10 @@
         if n > first:
             lax.fori_loop(first, n, step, 0)
 
+    def every(n, f, first=1):
+        for o in range(first, n):
+            f(o)
+
     def zz(o):
         return rem(z + o, Z)
 
@@ -127,6 +131,8 @@
     def th(o):
         return rem(h + o, H)
 
+    peers = [h, h + 1 - 2 * rem(h, 2), rem(h + 2, 4), 3 - h] if H == 4 else [th(o) for o in range(H)]
+
     barrier = pltpu.get_barrier_semaphore()
 
     def signal(dd, hh):
@@ -134,6 +140,10 @@
 
     for o in sorted(range(1, Z), key=lambda o: -min(o, Z - o)):
         signal(dz(o), h)
+    loc1 = pltpu.make_async_copy(x_hbm.at[:, yh, h], xs, sem_loc.at[0])
+    loc1c = pltpu.make_async_copy(x_hbm.at[:, oy, pl.ds(lo, H2)], xsc, sem_loc.at[1])
+    loc1.start()
+    loc1c.start()
     for o in range(1, XC):
         signal(block + tx(o), h)
     for o in range(XC):
@@ -145,10 +155,6 @@
         for o in range(XC):
             signal(block + o, hh)
 
-    loc1 = pltpu.make_async_copy(x_hbm.at[:, yh, h], xs, sem_loc.at[0])
-    loc1c = pltpu.make_async_copy(x_hbm.at[:, oy, pl.ds(lo, H2)], xsc, sem_loc.at[1])
-    loc1.start()
-    loc1c.start()
     ins = [
         pltpu.make_async_copy(w, wall.at[h, pl.ds(i * HW, HW)], sem_in.at[i])
         for i, w in enumerate((wq_hbm, wk_hbm, wv_hbm, wg_hbm))
@@ -175,9 +181,9 @@
 
     @pl.when(edge)
     def _():
-        each(Z, lambda o: a1c(o).start())
-
-    each(Z, lambda o: a1(o).start())
+        every(Z, lambda o: a1c(o).start())
+
+    every(Z, lambda o: a1(o).start())
     pl.semaphore_signal(ready, inc=1, device_id=(cross + xc, H - 1 - h), device_id_type=MESH)
     r1[z] = xs[z]
     r1c[z] = xsc[z]
@@ -191,10 +197,11 @@
     other = pl.ds(pl.multiple_of((1 - core) * WR, 16), WR)
 
     def aw(o):
-        hh = th(o)
+        hh = peers[o]
         return rcopy(wall.at[h, half], wall.at[h, half], sem_sw.at[hh], sem_rw.at[h], d, hh)
 
-    each(H, lambda o: aw(o).start())
+    for o in range(1, H):
+        aw(o).start()
 
     for copy in ins[5:]:
         copy.wait()
@@ -221,7 +228,7 @@
                 s2c[i, k, :, lanes] = v
 
             swap(r1c.at[:, i], tmp, store, Z, XC)
-            each(XC, lambda t: a2c(i, t).start(), 0)
+            every(XC, lambda t: a2c(i, t).start(), 0)
 
     each(Z, wait_r1)
 
@@ -234,15 +241,15 @@
         t = tx(o)
         return rcopy(s2.at[t], r2.at[yh, xc], sem_s2.at[t], sem_r2.at[yh * XC + xc], block + t, h)
 
-    each(XC, lambda o: a2(o).start())
+    every(XC, lambda o: a2(o).start())
     r2[yh, xc] = s2[xc]
 
     row = lax.broadcasted_iota(jnp.int32, (N, 1), 0)
     src = row // (2 * G)
-    mirror = (row // Z) % 2
+    mirror = (row // G) % 2
     src_h = jnp.where(mirror == 1, H - 1 - src % H, src % H)
     src_y = jnp.where(mirror == 1, oy, yh)
-    at = ((row % Z) * 2 + src_y) * (H * XC) + src_h * XC + (src // H) * 2 + (row // G) % 2
+    at = ((row % Z) * 2 + src_y) * (H * XC) + src_h * XC + (src // H) * 2 + (row // Z) % 2
     place[...] = jnp.where(lax.broadcasted_iota(jnp.int32, (N, N), 1) == at, 1.0, 0.0).astype(BF)
 
     def wait_r2(o):
@@ -256,20 +263,22 @@
     each(XC, wait_r2c, 0)
 
     def av(o):
-        hh = th(o)
+        hh = peers[o]
         return rcopy(wall.at[hh, half], wall.at[hh, half], sem_sv.at[hh], sem_rv.at[hh], sib, h)
 
     def pass_w(o):
-        hh = th(o)
+        hh = peers[o]
         rcopy(wall.at[hh, half], wall.at[hh, half], sem_sw.at[hh], sem_rw.at[hh], d, hh).wait_recv()
         av(o).start()
 
-    each(H, pass_w)
+    pass_w(1)
     activity = r2[...].astype(F32).reshape(S, CM)
     normed = standardize(activity, gain1_ref[...])
 
     for o in range(H):
-        hh = th(o)
+        hh = peers[o]
+        if 0 < o < H - 1:
+            pass_w(o + 1)
         if o > 0:
             rcopy(wall.at[hh, other], wall.at[hh, other], sem_sv.at[hh], sem_rv.at[hh], sib, h).wait_recv()
         proj = dot(wall[hh, : 4 * HW, :], normed, 1, 1)
@@ -291,7 +300,7 @@
         t = tx(o)
         return rcopy(acol.at[:, t], ra1.at[xc], sem_sa1.at[t], sem_ra1.at[xc], block + t, h)
 
-    each(XC, lambda o: aa1(o).start())
+    every(XC, lambda o: aa1(o).start())
     ra1[xc] = acol[:, xc]
 
     normed2 = standardize(after, gain2_ref[...])
@@ -306,26 +315,40 @@
         return rcopy(lcol, l1.at[Z + z], sem_sl1.at[Z + o], sem_rl1.at[Z + z], dm(o), H - 1 - h)
 
     pl.semaphore_wait(ready, 1)
-    each(Z, lambda o: al1m(o).start(), 0)
-    each(Z, lambda o: al1(o).start())
+    every(Z, lambda o: al1m(o).start(), 0)
+    every(Z, lambda o: al1(o).start())
     l1[z] = lcol[...]
 
     core_d = div(xc, H)
-    slot = h * H + rem(xc, H)
+    slot = rem(xc, H)
+    far = core != core_d
 
     def ar(o):
-        x2 = rem(xx + div(o, H), X)
-        return rcopy(rcol, right.at[slot], sem_sr.at[o], sem_rr.at[slot], block + 2 * x2 + core_d, th(rem(o, H)))
-
-    @pl.when(core == core_d)
-    def _():
-        right[slot] = rcol[...]
-
-    @pl.when(core != core_d)
-    def _():
-        ar(jnp.int32(0)).start()
-
-    each(X * H, lambda o: ar(o).start())
+        hh = th(o)
+        return rcopy(rcol, rights.at[h], sem_sr.at[hh], sem_rr.at[h], d, hh)
+
+    every(H, lambda o: ar(o).start())
+    rights[h] = rcol[...]
+
+    def ax1(o):
+        return rcopy(
+            rights, right.at[:, slot], sem_sq.at[o], sem_rq.at[slot], block + 2 * rem(xx + o, X) + core_d, h
+        )
+
+    def pass_right():
+        for o in range(1, H):
+            hh = th(o)
+            rcopy(rcol, rights.at[hh], sem_sr.at[hh], sem_rr.at[hh], d, hh).wait_recv()
+        for o in range(1, X):
+            ax1(o).start()
+
+        @pl.when(far)
+        def _():
+            ax1(0).start()
+
+        @pl.when(jnp.logical_not(far))
+        def _():
+            right[:, slot] = rights[...]
 
     def wait_a1(o):
         t = tx(o)
@@ -342,64 +365,81 @@
         t = zz(o)
         return rcopy(sa2.at[:, t], ra2.at[:, z], sem_sa2.at[t], sem_ra2.at[z], dz(o), h)
 
-    each(Z, lambda o: aa2(o).start())
+    every(Z, lambda o: aa2(o).start())
     ra2[:, z] = sa2[:, z]
 
     def aa3(t, o):
         return rcopy(
-            ra2.at[yh, t], o0_ref.at[t, yh, h], sem_sa3.at[o], sem_ra3.at[yh * H + h], block + xc, th(o)
+            ra2.at[yh, pl.ds(t, 2)], o0_ref.at[pl.ds(t, 2), yh, h], sem_sa3.at[o], sem_ra3.at[yh * H + h],
+            block + xc, th(o),
         )
 
     def aa3c(t, o):
         return rcopy(
-            ra2.at[oy, t], o0_ref.at[t, yh, h], sem_sa3.at[H + o], sem_ra3.at[yh * H + h], cross + xc, o
+            ra2.at[oy, pl.ds(t, 2)], o0_ref.at[pl.ds(t, 2), yh, h], sem_sa3.at[H + o], sem_ra3.at[yh * H + h],
+            cross + xc, o,
         )
 
-    def ring(t):
-        each(H, lambda o: aa3c(t, o).start(), 0)
-        each(H, lambda o: aa3(t, o).start())
-
-    def wait_a2(o):
-        t = zz(o)
-        rcopy(sa2.at[:, t], ra2.at[:, t], sem_sa2.at[t], sem_ra2.at[t], dz(o), h).wait_recv()
-        ring(t)
-
-    near = sorted(range(1, Z), key=lambda o: min(o, Z - o))
-    ring(z)
+    def wait_a2(t):
+        rcopy(sa2.at[:, t], ra2.at[:, t], sem_sa2.at[t], sem_ra2.at[t], d, h).wait_recv()
+
+    def ring(q):
+        t = 2 * rem(div(z, 2) + q, Z // 2)
+        if q == 0:
+            wait_a2(t + 1 - rem(z, 2))
+        else:
+            wait_a2(t)
+            wait_a2(t + 1)
+        for o in range(H):
+            aa3c(t, o).start()
+        for o in range(1, H):
+            aa3(t, o).start()
+
+    pass_right()
+    pairs = sorted(range(Z // 2), key=lambda q: min(q, Z // 2 - q))
+    ring(0)
 
     def wait_l1(k):
         rcopy(lcol, l1.at[k], sem_sl1.at[0], sem_rl1.at[k], d, h).wait_recv()
 
+    def al3(side):
+        part = left.at[side, :, core]
+        return rcopy(part, part, sem_sl3.at[side], sem_rl3.at[side], sib, h)
+
+    def wait_l3(side):
+        part = left.at[side, :, 1 - core]
+        rcopy(part, part, sem_sl3.at[side], sem_rl3.at[side], sib, h).wait_recv()
+
+    def left_side(side):
+        tmpl[...] = l1[side * Z : (side + 1) * Z].astype(F32).reshape(Z * CC, S)
+        for c in range(CC):
+            left[side, c, core] = tmpl[pl.ds(c, Z, stride=CC), :].astype(BF)
+        al3(side).start()
+
     each(Z, lambda o: wait_l1(zz(o)))
-    each(Z, lambda o: wait_l1(Z + o), 0)
-    tmpl[...] = l1[...].astype(F32).reshape(G * CC, S)
-    for c in range(CC):
-        left[0, c] = tmpl[pl.ds(c, G, stride=CC), :].astype(BF)
-    al3 = rcopy(left.at[0], left.at[1], sem_sl3, sem_rl3, sib, h)
-    al3.start()
-
-    for k in range(X * H):
-        from_h, from_xc = k // H, core * H + k % H
-
-        @pl.when(jnp.logical_not((from_h == h) & (from_xc == xc)))
+    left_side(0)
+
+    for k in range(H):
+        from_xc = core * H + k
+
+        @pl.when(from_xc != xc)
         def _():
-            rcopy(rcol, right.at[k], sem_sr.at[0], sem_rr.at[k], block + from_xc, from_h).wait_recv()
+            rcopy(rights, right.at[:, k], sem_sq.at[0], sem_rq.at[k], block + from_xc, h).wait_recv()
 
     own = xx * H + h
 
     def ax(side, x2, hh):
         k = (side * X + x2) * H + hh
-        at_core = core if side == 0 else 1 - core
         return rcopy(
-            res.at[side, x2 * H + hh], rx.at[own, at_core], sem_sx.at[k], sem_rx.at[own * 2 + at_core],
+            res.at[side, x2 * H + hh], rx.at[own, side], sem_sx.at[k], sem_rx.at[own * 2 + side],
             block + 2 * x2 + core, hh,
         )
 
     def pair_half(side):
-        lefts = left[side].reshape(CC * G, S)
+        lefts = left[side].astype(F32).reshape(CC * G, S).astype(BF)
         flats = []
         for x2 in range(X):
-            outer = dot(lefts, right[x2 * H : (x2 + 1) * H].reshape(H * CC, S), 1, 1) * (1.0 / S)
+            outer = dot(lefts, right[x2].reshape(H * CC, S), 1, 1) * (1.0 / S)
             flat = [[] for _ in range(H)]
             for c in range(0, CC, H):
                 for k, part in enumerate(turn([outer[(c + r) * G : (c + r + 1) * G] for r in range(H)])):
@@ -414,20 +454,23 @@
 
                 @pl.when(here)
                 def _():
-                    rx[own, core if side == 0 else 1 - core] = res[side, x2 * H + hh]
+                    rx[own, side] = res[side, x2 * H + hh]
 
                 @pl.when(jnp.logical_not(here))
                 def _():
                     ax(side, x2, hh).start()
 
-    for o in near[:4]:
-        wait_a2(o)
+    for q in pairs[1:3]:
+        ring(q)
+    wait_l3(0)
     pair_half(0)
-    for o in near[4:]:
-        wait_a2(o)
+    for q in pairs[3:]:
+        ring(q)
+
+    each(Z, lambda o: wait_l1(Z + o), 0)
+    left_side(1)
     o0_ref[:, yh, h] = ra2[yh]
-
-    rcopy(left.at[0], left.at[1], sem_sl3, sem_rl3, sib, h).wait_recv()
+    wait_l3(1)
     pair_half(1)
 
     for x2 in range(X):
@@ -460,20 +503,25 @@
         for i in range(H2):
             each(XC, lambda t: a2c(i, t).wait_send(), 0)
 
-    each(H, lambda o: aw(o).wait_send())
-    each(H, lambda o: av(o).wait_send())
+    for o in range(1, H):
+        aw(o).wait_send()
+        av(o).wait_send()
     each(XC, lambda o: a2(o).wait_send())
     each(Z, lambda o: al1m(o).wait_send(), 0)
     each(Z, lambda o: al1(o).wait_send())
 
-    @pl.when(core != core_d)
+    each(H, lambda o: ar(o).wait_send())
+    for o in range(1, X):
+        ax1(o).wait_send()
+
+    @pl.when(far)
     def _():
-        ar(jnp.int32(0)).wait_send()
-
-    each(X * H, lambda o: ar(o).wait_send())
+        ax1(0).wait_send()
+
     each(XC, lambda o: aa1(o).wait_send())
     each(Z, lambda o: aa2(o).wait_send())
-    al3.wait_send()
+    al3(0).wait_send()
+    al3(1).wait_send()
     for side in range(2):
         for x2 in range(X):
             for hh in range(H):
@@ -516,9 +564,10 @@
         pltpu.VMEM((CC, S), BF),
         pltpu.VMEM((CC, S), BF),
         pltpu.VMEM((G, CC, S), BF),
-        pltpu.VMEM((G * CC, S), F32),
-        pltpu.VMEM((2, CC, G, S), BF),
-        pltpu.VMEM((X * H, CC, S), BF),
+        pltpu.VMEM((Z * CC, S), F32),
+        pltpu.VMEM((2, CC, 2, Z, S), BF),
+        pltpu.VMEM((H, CC, S), BF),
+        pltpu.VMEM((X, H, CC, S), BF),
         pltpu.VMEM((2, X * H, G, CZ), BF),
         pltpu.VMEM((X * H, 2, G, CZ), BF),
         pltpu.VMEM((XC, 2, Z, CM), BF),
@@ -528,7 +577,7 @@
     ]
     sems = [
         Z, Z, Z, Z, H, H, H, H, XC, H // 2 * XC, 2 * XC, G, G,
-        None, None, X * H, X * H, XC, XC, Z, Z, 2 * H, 2 * H, 2 * X * H, 2 * X * H,
+        2, 2, H, H, X, H, XC, XC, Z, Z, 2 * H, 2 * H, 2 * X * H, 2 * X * H,
         2, 11,
     ]
     scratch += [dma if n is None else dma((n,)) for n in sems]

time: 52.8 us -> 52.4 us (level)
  no operation moved by 1% of the time
where the time goes in v5:
time: 52.4 us; the launch traced here: 52.2 us
  Pallas kernels  50.2 us (96%)
  local copies, waits for them, and re-layouts  1.36 us (3%)
  between operations  0.64 us (1%)
    pallas_call x1, Pallas kernels, shards(): pl.pallas_call(functools.partial(kernel, (Z, H, CM)), out_shape=(pltpu.VM...  50.2 us
    unnamed x2, local copies, waits for them, and re-layouts  1.36 us

profile of v5, /device:TPU:1, one launch (start us, length us, event | category | flops | bytes accessed | tf_op | source)
XLA Modules:
  0.0 52.2 jit_solution(8475967586557296239)
XLA Ops:
  0.6 50.2 %shard_map.131 = (bf16[8,2,4,8,256]{4,3,2,1,0:T(8,128)(2,1)S(1)}, bf16[128,512]{1,0:T(8,128)(2,1)S(1)}) custom-call(bf16[8,2,4,8,256]{4,3,2,1,0:T(8,128)(2,1)} %bitcast.16, bf16[64,256]{1,0:T(8,128)(2,1)} %bitcast.17, bf16[64,256]{1,0:T(8,128)(2,1)} %bitcast.18, bf16[64,256]{1,0:T(8,128)(2,1)} %bitcast.19, bf16[64,256]{1,0:T(8,128)(2,1)} %bitcast.20, ...), custom_call_target="tpu_custom_call" | custom-call | tf_op jit(solution)/shard_map/pallas_call | solution.py:585
  50.9 0.7 %copy.16 = bf16[1,512,256]{2,1,0:T(8,128)(2,1)} copy(bf16[1,512,256]{2,1,0:T(8,128)(2,1)S(1)} %bitcast.14) | data formatting | bytes 524288
  51.6 0.7 %copy.17 = bf16[512,4,32]{0,2,1:T(8,128)(2,1)} copy(bf16[512,4,32]{0,2,1:T(8,128)(2,1)S(1)} %bitcast.15) | data formatting | bytes 262144

commit v6 on v5

--- a/solution.py
+++ b/solution.py
@@ -116,6 +116,8 @@
         for o in range(first, n):
             f(o)
 
+    distant = sorted(range(Z), key=lambda o: -min(o, Z - o))
+
     def zz(o):
         return rem(z + o, Z)
 
@@ -181,9 +183,11 @@
 
     @pl.when(edge)
     def _():
-        every(Z, lambda o: a1c(o).start())
-
-    every(Z, lambda o: a1(o).start())
+        for o in distant[:-1]:
+            a1c(o).start()
+
+    for o in distant[:-1]:
+        a1(o).start()
     pl.semaphore_signal(ready, inc=1, device_id=(cross + xc, H - 1 - h), device_id_type=MESH)
     r1[z] = xs[z]
     r1c[z] = xsc[z]
@@ -315,8 +319,10 @@
         return rcopy(lcol, l1.at[Z + z], sem_sl1.at[Z + o], sem_rl1.at[Z + z], dm(o), H - 1 - h)
 
     pl.semaphore_wait(ready, 1)
-    every(Z, lambda o: al1m(o).start(), 0)
-    every(Z, lambda o: al1(o).start())
+    for o in distant:
+        al1m(o).start()
+    for o in distant[:-1]:
+        al1(o).start()
     l1[z] = lcol[...]
 
     core_d = div(xc, H)
@@ -365,7 +371,8 @@
         t = zz(o)
         return rcopy(sa2.at[:, t], ra2.at[:, z], sem_sa2.at[t], sem_ra2.at[z], dz(o), h)
 
-    every(Z, lambda o: aa2(o).start())
+    for o in distant[:-1]:
+        aa2(o).start()
     ra2[:, z] = sa2[:, z]
 
     def aa3(t, o):

time: 52.4 us -> 52.2 us (level)
  no operation moved by 1% of the time
where the time goes in v6:
time: 52.2 us; the launch traced here: 52.1 us
  Pallas kernels  50.1 us (96%)
  local copies, waits for them, and re-layouts  1.36 us (3%)
  between operations  0.64 us (1%)
    pallas_call x1, Pallas kernels, shards(): pl.pallas_call(functools.partial(kernel, (Z, H, CM)), out_shape=(pltpu.VM...  50.1 us
    unnamed x2, local copies, waits for them, and re-layouts  1.36 us

profile of v6, /device:TPU:1, one launch (start us, length us, event | category | flops | bytes accessed | tf_op | source)
XLA Modules:
  0.0 52.1 jit_solution(17274952910508473089)
XLA Ops:
  0.6 50.1 %shard_map.131 = (bf16[8,2,4,8,256]{4,3,2,1,0:T(8,128)(2,1)S(1)}, bf16[128,512]{1,0:T(8,128)(2,1)S(1)}) custom-call(bf16[8,2,4,8,256]{4,3,2,1,0:T(8,128)(2,1)} %bitcast.16, bf16[64,256]{1,0:T(8,128)(2,1)} %bitcast.17, bf16[64,256]{1,0:T(8,128)(2,1)} %bitcast.18, bf16[64,256]{1,0:T(8,128)(2,1)} %bitcast.19, bf16[64,256]{1,0:T(8,128)(2,1)} %bitcast.20, ...), custom_call_target="tpu_custom_call" | custom-call | tf_op jit(solution)/shard_map/pallas_call | solution.py:592
  50.7 0.7 %copy.16 = bf16[1,512,256]{2,1,0:T(8,128)(2,1)} copy(bf16[1,512,256]{2,1,0:T(8,128)(2,1)S(1)} %bitcast.14) | data formatting | bytes 524288
  51.4 0.7 %copy.17 = bf16[512,4,32]{0,2,1:T(8,128)(2,1)} copy(bf16[512,4,32]{0,2,1:T(8,128)(2,1)S(1)} %bitcast.15) | data formatting | bytes 262144
